TPU v7x, 256 devices: a whole 4x4x8 slice. The times are simulated.
256 devices in a mesh: dp: 8 (over x, y_hi), tensor: 32 (over y_lo, z, core).
Axes of the slice: x: 4, y: 4 (y_hi: 2, y_lo: 2; y = y_hi * 2 + y_lo), z: 8, core: 2. Of those that a mesh axis runs over, the one named last changes fastest.
Arguments:
- tokens: bfloat16 [512, 16384], P('tensor', 'dp'), may hold values from -6 to 6
- gate_codes: int32 [4096, 53248], P('dp', 'tensor'), may hold values from 0 to 4095
- gate_scales: bfloat16 [128, 53248], P('dp', 'tensor'), may hold values from 0.00093460083 to 0.0078125
- up_codes: int32 [4096, 53248], P('dp', 'tensor'), may hold values from 0 to 4095
- up_scales: bfloat16 [128, 53248], P('dp', 'tensor'), may hold values from 0.00093460083 to 0.0078125
- down_codes: int32 [13312, 16384], P('tensor', 'dp'), may hold values from 0 to 4095
- down_scales: bfloat16 [416, 16384], P('tensor', 'dp'), may hold values from 0.0005187988 to 0.004333496
- flip_signs: int32 [53248], P('tensor'), may hold values from 0 to 1
Outputs:
- ffn_out: bfloat16 [512, 16384], P('tensor', 'dp')
Inputs may be any that keep to these rules, and one draw needn't show every extreme that they name: `gate_codes`: each word holds four 3-bit codes: bits 3 j to 3 j + 2 that of row 4 i + j. `up_codes`: each word holds four 3-bit codes: bits 3 j to 3 j + 2 that of row 4 i + j. `down_codes`: each word holds four 3-bit codes: bits 3 j to 3 j + 2 that of hidden unit 4 i + j. `flip_signs`: 1 stands for plus one, 0 for minus one.
All inputs are finite; a program needn't handle non-finite values.
Results may differ from a plain program's by a relative error of at most 0.04.
Values may be sent and summed in bfloat16 or wider, within the bound.
A program may use at most 128 MiB of HBM per device.

v0:
```python
import jax
import jax.numpy as jnp
import numpy as np
from jax import lax
from jax.sharding import PartitionSpec as P

FF = 53248
KB = 52
BLK = 32
GQ = 128


def from_partner(value, axis, bit):
    return lax.ppermute(value, axis, [(i, i ^ 1 << bit) for i in range(lax.axis_size(axis))])


def paley_table():
    field_square = np.zeros(25, dtype=np.int64)
    for first_part in range(5):
        for second_part in range(5):
            if first_part == 0 and second_part == 0:
                continue
            real_part = (first_part * first_part + 2 * second_part * second_part) % 5
            root_part = 2 * first_part * second_part % 5
            field_square[real_part + 5 * root_part] = 1
    character = np.where(field_square == 1, 1, -1)
    character[0] = 0
    jacobsthal = np.zeros((25, 25), dtype=np.int64)
    for left_item in range(25):
        for right_item in range(25):
            diff_real = (left_item % 5 - right_item % 5) % 5
            diff_root = (left_item // 5 - right_item // 5) % 5
            jacobsthal[left_item, right_item] = character[diff_real + 5 * diff_root]
    conference = np.zeros((26, 26), dtype=np.int64)
    conference[0, 1:] = 1
    conference[1:, 0] = 1
    conference[1:, 1:] = jacobsthal
    outer_part = np.array([[1, -1], [-1, -1]], dtype=np.int64)
    inner_part = np.array([[1, 1], [1, -1]], dtype=np.int64)
    return (
        np.kron(conference, outer_part) + np.kron(np.eye(26, dtype=np.int64), inner_part)
    ).astype(np.float32)


def sylvester_static(order_size):
    position = np.arange(order_size)
    parity = np.zeros((order_size, order_size), dtype=np.int64)
    for bit_place in range(max(order_size.bit_length() - 1, 0)):
        parity = parity + (position[:, None] >> bit_place & position[None, :] >> bit_place & 1)
    return (1 - 2 * (parity & 1)).astype(np.float32)


def sylvester(order_size):
    return jnp.asarray(sylvester_static(order_size), dtype=jnp.float32)


def dequant(code_words, scales, group_size):
    shifts = 3 * jnp.arange(4, dtype=jnp.int32)
    nibbles = jnp.bitwise_and(jnp.right_shift(code_words[:, None, :], shifts[None, :, None]), 7)
    levels = nibbles.reshape(4 * code_words.shape[0], code_words.shape[1]) - 4
    spread = jnp.repeat(scales.astype(jnp.float32), group_size, axis=0)
    return (levels.astype(jnp.float32) * spread).astype(jnp.bfloat16)


def per_device(
    tokens, gate_codes, gate_scales, up_codes, up_scales, down_codes, down_scales, flip_signs
):
    gate_weight = dequant(gate_codes, gate_scales, GQ)
    up_weight = dequant(up_codes, up_scales, GQ)
    width_here = gate_weight.shape[1]
    both_weights = jnp.concatenate([gate_weight, up_weight], axis=1)
    all_rows = lax.all_gather(tokens, "tensor", axis=0, tiled=True)
    summed = lax.psum_scatter(
        jnp.dot(all_rows, both_weights, preferred_element_type=jnp.float32).astype(jnp.bfloat16),
        "dp",
        scatter_dimension=0,
        tiled=True,
    ).astype(jnp.float32)
    hidden = (jax.nn.silu(summed[:, :width_here]) * summed[:, width_here:]).astype(jnp.bfloat16)
    flipped = jnp.where(flip_signs[None, :] == 1, hidden, -hidden)
    local_groups = width_here // (KB * BLK)
    row_total = flipped.shape[0]
    block_table = jnp.asarray(np.kron(paley_table(), sylvester_static(BLK)), dtype=jnp.bfloat16)
    inner = jnp.dot(flipped, block_table, preferred_element_type=jnp.float32)
    mixed_rows = jnp.einsum(
        "tgc,gh->thc",
        inner.reshape(row_total, local_groups, KB * BLK),
        sylvester(local_groups),
        precision=lax.Precision.HIGHEST,
    ).reshape(row_total, width_here)
    bit_total = lax.axis_size("tensor").bit_length() - 1
    my_place = lax.axis_index("tensor")
    section_list = list(range(bit_total))
    for bit_place in section_list:
        partner = from_partner(mixed_rows.astype(jnp.bfloat16), "tensor", bit_place).astype(
            mixed_rows.dtype
        )
        upper_half = jnp.bitwise_and(jnp.right_shift(my_place, bit_place), 1) == 1
        mixed_rows = jnp.where(upper_half, partner - mixed_rows, mixed_rows + partner)
    rotated = (mixed_rows * FF ** (-0.5)).astype(jnp.bfloat16)
    down_weight = dequant(down_codes, down_scales, GQ)
    terms = jnp.dot(
        lax.all_gather(rotated, "dp", axis=0, tiled=True),
        down_weight,
        preferred_element_type=jnp.float32,
    )
    return lax.psum_scatter(terms.astype(jnp.bfloat16), "tensor", scatter_dimension=0, tiled=True)


def solution(mesh):
    return jax.shard_map(
        per_device,
        mesh=mesh,
        in_specs=(
            P("tensor", "dp"),
            P("dp", "tensor"),
            P("dp", "tensor"),
            P("dp", "tensor"),
            P("dp", "tensor"),
            P("tensor", "dp"),
            P("tensor", "dp"),
            P("tensor"),
        ),
        out_specs=P("tensor", "dp"),
        check_vma=False,
    )
```

profile of v0, /device:TPU:2, one launch (start us, length us, event | category | flops | bytes accessed | tf_op | source)
XLA Modules:
  0.0 416.3 jit_solution(17982547667729905335)
XLA Ops:
  6.5 0.0 all-gather.3.cloned.1.call-start
  6.5 0.7 all-gather.3.cloned.1.call-update
  7.3 0.0 reduce-scatter.7.cloned.1.call-start
  7.3 0.2 shift_right_arithmetic.83
  7.5 9.1 %shift_right_arithmetic.80 = s32[512,4,1664]{2,1,0:T(4,128)} broadcast(s32[512,1664]{1,0:T(8,128)} %param.11), dimensions={0,2} | broadcast | bytes 17039360 | tf_op jit(solution)/shard_map/shift_right_arithmetic | solution.py:59
  16.6 16.8 %shift_right_arithmetic.81 = s32[2048,1664]{1,0:T(8,128)} reshape(s32[512,4,1664]{2,1,0:T(4,128)} %shift_right_arithmetic.80) | data formatting | bytes 27262976 | tf_op jit(solution)/shard_map/shift_right_arithmetic | solution.py:59
  33.4 0.0 copy-done
  33.4 7.2 %shift_right_arithmetic.86 = s32[512,4,1664]{2,1,0:T(4,128)} broadcast(s32[512,1664]{1,0:T(8,128)S(1)} %copy-done), dimensions={0,2} | broadcast | bytes 17039360 | tf_op jit(solution)/shard_map/shift_right_arithmetic | solution.py:59
  40.6 16.6 %shift_right_arithmetic.87 = s32[2048,1664]{1,0:T(8,128)} reshape(s32[512,4,1664]{2,1,0:T(4,128)} %shift_right_arithmetic.86) | data formatting | bytes 27262976 | tf_op jit(solution)/shard_map/shift_right_arithmetic | solution.py:59
  57.2 0.0 copy-done.2
  57.2 0.0 copy-done.3
  57.3 15.3 %fusion.6 = (bf16[2048,1664]{1,0:T(8,128)(2,1)}, bf16[2048,1664]{1,0:T(8,128)(2,1)}) fusion(s32[2048,1664]{1,0:T(8,128)} %shift_right_arithmetic.81, f32[16,1664]{1,0:T(8,128)S(1)} %convert_element_type.76, s32[2048]{0:T(1024)S(1)} %shift_right_arithmetic.83, f32[16,1664]{1,0:T(8,128)S(1)} %convert_element_type.79, s32[2048,1664]{1,0:T(8,128)} %shift_right_arithmetic.87), kind=kLoop, calls=%fused_computation.9 | loop fusion | flops 40894464 | bytes 41115648 | tf_op jit(solution)/shard_map/convert_element_type | solution.py:62
  72.5 4.4 %all-gather.3.cloned.1.call-done = bf16[512,2048]{1,0:T(8,128)(2,1)} async-done(((bf16[16,2048]{1,0:T(8,128)(2,1)}), bf16[512,2048]{1,0:T(8,128)(2,1)}) %all-gather.3.cloned.1.call-update) | async-done | bytes 2097168 | tf_op jit(solution)/shard_map/all_gather | solution.py:72
  76.9 12.8 %fusion.10 = bf16[512,3328]{0,1:T(8,128)(2,1)S(1)} fusion(bf16[512,2048]{1,0:T(8,128)(2,1)} %all-gather.3.cloned.1.call-done, bf16[2048,1664]{1,0:T(8,128)(2,1)} %get-tuple-element.8, bf16[2048,1664]{1,0:T(8,128)(2,1)} %get-tuple-element.7), kind=kOutput, calls=%fused_computation.11 | convolution fusion | flops 7008288768 | bytes 19136512 | tf_op jit(solution)/shard_map/dot_general | solution.py:74
  89.7 3.8 copy.11
  93.5 0.0 reduce-scatter.7.cloned.1.call-update
  93.5 0.0 all-gather.5.cloned.1.call-start
  93.6 0.0 copy-done.4
  93.6 86.1 %reduce-scatter.7.cloned.1.call-done = bf16[64,3328]{1,0:T(8,128)(2,1)} async-done(((bf16[512,3328]{1,0:T(8,128)(2,1)}), bf16[64,3328]{1,0:T(8,128)(2,1)}) %reduce-scatter.7.cloned.1.call-update) | async-done | bytes 426000
  179.7 1.4 copy.12
  181.1 0.1 convert_element_type.83
  181.2 3.8 fusion.29
  185.0 0.1 collective-permute-start
  185.1 1.4 collective-permute-done
  186.6 0.1 fusion.24
  186.6 1.7 collective-permute-start.1
  188.3 5.7 %collective-permute-done.1 = bf16[64,1664]{1,0:T(8,128)(2,1)S(1)} collective-permute-done((bf16[64,1664]{1,0:T(8,128)(2,1)S(1)}, bf16[64,1664]{1,0:T(8,128)(2,1)S(1)}, u32[]{:S(2)}, u32[]{:S(2)}) %collective-permute-start.1) | collective-permute-done | bytes 213024 | tf_op jit(solution)/shard_map/ppermute | solution.py:14
  194.0 0.1 fusion.23
  194.2 2.6 collective-permute-start.2
  196.8 9.4 %collective-permute-done.2 = bf16[64,1664]{1,0:T(8,128)(2,1)S(1)} collective-permute-done((bf16[64,1664]{1,0:T(8,128)(2,1)S(1)}, bf16[64,1664]{1,0:T(8,128)(2,1)S(1)}, u32[]{:S(2)}, u32[]{:S(2)}) %collective-permute-start.2) | collective-permute-done | bytes 213024 | tf_op jit(solution)/shard_map/ppermute | solution.py:14
  206.2 0.2 fusion.27
  206.4 5.9 %collective-permute-start.3 = (bf16[64,1664]{1,0:T(8,128)(2,1)S(1)}, bf16[64,1664]{1,0:T(8,128)(2,1)S(1)}, u32[]{:S(2)}, u32[]{:S(2)}) collective-permute-start(bf16[64,1664]{1,0:T(8,128)(2,1)S(1)} %get-tuple-element.5), channel_id=1, source_target_pairs={{0,8},{1,9},{2,10},{3,11},{4,12},{5,13},{6,14},{7,15},{8,0},{9,1},... | collective-permute-start | bytes 638984 | tf_op jit(solution)/shard_map/ppermute | solution.py:14
  212.2 8.3 %collective-permute-done.3 = bf16[64,1664]{1,0:T(8,128)(2,1)S(1)} collective-permute-done((bf16[64,1664]{1,0:T(8,128)(2,1)S(1)}, bf16[64,1664]{1,0:T(8,128)(2,1)S(1)}, u32[]{:S(2)}, u32[]{:S(2)}) %collective-permute-start.3) | collective-permute-done | bytes 213024 | tf_op jit(solution)/shard_map/ppermute | solution.py:14
  220.5 0.1 fusion.22
  220.6 0.7 collective-permute-start.4
  221.3 5.7 %collective-permute-done.4 = bf16[64,1664]{1,0:T(8,128)(2,1)S(1)} collective-permute-done((bf16[64,1664]{1,0:T(8,128)(2,1)S(1)}, bf16[64,1664]{1,0:T(8,128)(2,1)S(1)}, u32[]{:S(2)}, u32[]{:S(2)}) %collective-permute-start.4) | collective-permute-done | bytes 213024 | tf_op jit(solution)/shard_map/ppermute | solution.py:14
  227.0 0.8 fusion.20
  227.8 0.0 all-gather.5.cloned.1.call-update
  227.8 0.0 reduce-scatter.5.cloned.1.call-start
  227.9 0.1 shift_right_arithmetic.92
  228.0 9.0 %shift_right_arithmetic.89 = s32[416,4,2048]{2,1,0:T(4,128)} broadcast(s32[416,2048]{1,0:T(8,128)} %param.15), dimensions={0,2} | broadcast | bytes 17039360 | tf_op jit(solution)/shard_map/shift_right_arithmetic | solution.py:59
  237.1 16.8 %shift_right_arithmetic.90 = s32[1664,2048]{1,0:T(8,128)} reshape(s32[416,4,2048]{2,1,0:T(4,128)} %shift_right_arithmetic.89) | data formatting | bytes 27262976 | tf_op jit(solution)/shard_map/shift_right_arithmetic | solution.py:59
  253.9 0.0 copy-done.1
  253.9 10.1 %fusion.4 = bf16[1664,2048]{1,0:T(8,128)(2,1)} fusion(s32[1664,2048]{1,0:T(8,128)} %shift_right_arithmetic.90, f32[13,2048]{1,0:T(8,128)S(1)} %convert_element_type.97, s32[1664]{0:T(1024)S(1)} %shift_right_arithmetic.92), kind=kLoop, calls=%fused_computation.5 | loop fusion | flops 20447232 | bytes 20560384 | tf_op jit(solution)/shard_map/convert_element_type | solution.py:62
  263.9 19.2 %all-gather.5.cloned.1.call-done = bf16[512,1664]{1,0:T(8,128)(2,1)} async-done(((bf16[64,1664]{1,0:T(8,128)(2,1)}), bf16[512,1664]{1,0:T(8,128)(2,1)}) %all-gather.5.cloned.1.call-update) | async-done | bytes 1703952 | tf_op jit(solution)/shard_map/all_gather | solution.py:103
  283.2 8.8 %convolution_convert_fusion = bf16[512,2048]{1,0:T(8,128)(2,1)} fusion(bf16[512,1664]{1,0:T(8,128)(2,1)} %all-gather.5.cloned.1.call-done, bf16[1664,2048]{1,0:T(8,128)(2,1)} %fusion.4), kind=kOutput, calls=%fused_computation.12 | convolution fusion | flops 3490709504 | bytes 10616832 | tf_op jit(solution)/shard_map/dot_general | solution.py:102
  291.9 0.0 reduce-scatter.5.cloned.1.call-update
  291.9 117.8 %reduce-scatter.5.cloned.1.call-done = bf16[16,2048]{1,0:T(8,128)(2,1)} async-done(((bf16[512,2048]{1,0:T(8,128)(2,1)}), bf16[16,2048]{1,0:T(8,128)(2,1)}) %reduce-scatter.5.cloned.1.call-update) | async-done | bytes 65552 | tf_op jit(solution)/shard_map/reduce_scatter | solution.py:107
  (12 shorter events, 0.1 us)
Async XLA Ops:
  6.5 70.4 %all-gather.3.cloned.1.call-start = ((), (), s32[]{:S(2)}) async-start(), calls=%async_computation.2 | async-start | bytes 2162688 | tf_op jit(solution)/shard_map/all_gather | solution.py:72
  7.3 172.4 %reduce-scatter.7.cloned.1.call-start = ((), (), s32[]{:S(2)}) async-start(), calls=%async_computation.5 | async-start | bytes 3833856
  16.6 16.8 %copy-start = (s32[512,1664]{1,0:T(8,128)S(1)}, s32[512,1664]{1,0:T(8,128)}, u32[]{:S(2)}) copy-start(s32[512,1664]{1,0:T(8,128)} %param.13) | copy-start | bytes 10223620
  40.6 16.6 %copy-start.2 = (bf16[16,1664]{1,0:T(8,128)(2,1)S(1)}, bf16[16,1664]{1,0:T(8,128)(2,1)}, u32[]{:S(2)}) copy-start(bf16[16,1664]{1,0:T(8,128)(2,1)} %param.12) | copy-start | bytes 159748
  40.6 16.6 %copy-start.3 = (bf16[16,1664]{1,0:T(8,128)(2,1)S(1)}, bf16[16,1664]{1,0:T(8,128)(2,1)}, u32[]{:S(2)}) copy-start(bf16[16,1664]{1,0:T(8,128)(2,1)} %param.14) | copy-start | bytes 159748
  76.9 16.7 %copy-start.4 = (s32[1664]{0:T(1024)S(1)}, s32[1664]{0:T(1024)}, u32[]{:S(2)}) copy-start(s32[1664]{0:T(1024)} %param.17) | copy-start | bytes 19972
  93.5 189.6 %all-gather.5.cloned.1.call-start = ((), (), s32[]{:S(2)}) async-start(), calls=%async_computation.3 | async-start | bytes 1916928 | tf_op jit(solution)/shard_map/all_gather | solution.py:103
  185.0 1.6 collective-permute-start
  186.6 7.4 %collective-permute-start.1 = (bf16[64,1664]{1,0:T(8,128)(2,1)S(1)}, bf16[64,1664]{1,0:T(8,128)(2,1)S(1)}, u32[]{:S(2)}, u32[]{:S(2)}) collective-permute-start(bf16[64,1664]{1,0:T(8,128)(2,1)S(1)} %fusion.24), channel_id=1, source_target_pairs={{0,2},{1,3},{2,0},{3,1},{4,6},{5,7},{6,4},{7,5},{8,10},{9,11},{10,... | collective-permute-start | bytes 638984 | tf_op jit(solution)/shard_map/ppermute | solution.py:14
  194.2 12.0 %collective-permute-start.2 = (bf16[64,1664]{1,0:T(8,128)(2,1)S(1)}, bf16[64,1664]{1,0:T(8,128)(2,1)S(1)}, u32[]{:S(2)}, u32[]{:S(2)}) collective-permute-start(bf16[64,1664]{1,0:T(8,128)(2,1)S(1)} %fusion.23), channel_id=1, source_target_pairs={{0,4},{1,5},{2,6},{3,7},{4,0},{5,1},{6,2},{7,3},{8,12},{9,13},{10,... | collective-permute-start | bytes 638984 | tf_op jit(solution)/shard_map/ppermute | solution.py:14
  206.4 14.2 %collective-permute-start.3 = (bf16[64,1664]{1,0:T(8,128)(2,1)S(1)}, bf16[64,1664]{1,0:T(8,128)(2,1)S(1)}, u32[]{:S(2)}, u32[]{:S(2)}) collective-permute-start(bf16[64,1664]{1,0:T(8,128)(2,1)S(1)} %get-tuple-element.5), channel_id=1, source_target_pairs={{0,8},{1,9},{2,10},{3,11},{4,12},{5,13},{6,14},{7,15},{8,0},{9,1},... | collective-permute-start | bytes 638984 | tf_op jit(solution)/shard_map/ppermute | solution.py:14
  220.6 6.4 %collective-permute-start.4 = (bf16[64,1664]{1,0:T(8,128)(2,1)S(1)}, bf16[64,1664]{1,0:T(8,128)(2,1)S(1)}, u32[]{:S(2)}, u32[]{:S(2)}) collective-permute-start(bf16[64,1664]{1,0:T(8,128)(2,1)S(1)} %fusion.22), channel_id=1, source_target_pairs={{0,16},{1,17},{2,18},{3,19},{4,20},{5,21},{6,22},{7,23},{8,24},{9,... | collective-permute-start | bytes 638984 | tf_op jit(solution)/shard_map/ppermute | solution.py:14
  227.8 182.0 %reduce-scatter.5.cloned.1.call-start = ((), (), s32[]{:S(2)}) async-start(), calls=%async_computation.4 | async-start | bytes 2162688 | tf_op jit(solution)/shard_map/reduce_scatter | solution.py:107
  237.1 16.8 %copy-start.1 = (bf16[13,2048]{1,0:T(8,128)(2,1)S(1)}, bf16[13,2048]{1,0:T(8,128)(2,1)}, u32[]{:S(2)}) copy-start(bf16[13,2048]{1,0:T(8,128)(2,1)} %param.16) | copy-start | bytes 159748
Sparse Core Ops, SparseCore 0:
  9.2 67.6 all-gather.2
  93.7 85.9 reduce-scatter.6
  227.9 55.1 all-gather.4
  292.1 117.6 reduce-scatter.4
where the time goes:
time: 418 us; the launch traced here: 416 us
  waiting for transfers between devices  259 us (62%)
  local copies, waits for them, and re-layouts  81.1 us (19%)
  other arithmetic  26.8 us (6%)
  matrix products  25.4 us (6%)
  between operations  13.3 us (3%)
  starting transfers between devices  11.1 us (3%)
    reduce_scatter x1, waiting for transfers between devices, per_device(): lax.psum_scatter(terms.astype(jnp.bfloat16), 'tensor', scatter_dimension=...  118 us
    unnamed x5, waiting for transfers between devices  86.8 us
    shift_right_arithmetic x10, local copies, waits for them, and re-layouts, dequant(): jnp.right_shift(code_words[:, None, :], shifts[None, :, None])  75.9 us
    ppermute x5, waiting for transfers between devices, from_partner(): lax.ppermute(value, axis, [(i, i ^ 1 << bit) for i in range(lax.axis_size...  30.5 us
    convert_element_type x2, other arithmetic, dequant(): return (levels.astype(jnp.float32) * spread).astype(jnp.bfloat16)  25.4 us
    all_gather x1, waiting for transfers between devices, per_device(): lax.all_gather(rotated, 'dp', axis=0, tiled=True)  19.2 us
    dot_general x1, matrix products, per_device(): jnp.dot(all_rows, both_weights, preferred_element_type=jnp.float32)  12.8 us
    ppermute x5, starting transfers between devices, from_partner(): lax.ppermute(value, axis, [(i, i ^ 1 << bit) for i in range(lax.axis_size...  11 us
  transfers between devices with their start and end apart: 9, of which 9 were waited for; matrix products, arithmetic and copies ran while one was open for 24% of the time, Pallas kernels for 0%

commit v1 on v0

v1 whole, which is shorter than its diff:
```python
import functools

import jax
import jax.numpy as jnp
import numpy as np
from jax import lax
from jax.experimental import pallas as pl
from jax.experimental.pallas import tpu as pltpu
from jax.sharding import PartitionSpec as P

FF = 53248
KB = 52
BLK = 32
MESH = pl.DeviceIdType.MESH
BF16 = jnp.bfloat16
F32 = jnp.float32
VMEM_LIMIT = 60 * 1024 * 1024


def paley_table():
    field_square = np.zeros(25, dtype=np.int64)
    for first_part in range(5):
        for second_part in range(5):
            if first_part == 0 and second_part == 0:
                continue
            real_part = (first_part * first_part + 2 * second_part * second_part) % 5
            root_part = 2 * first_part * second_part % 5
            field_square[real_part + 5 * root_part] = 1
    character = np.where(field_square == 1, 1, -1)
    character[0] = 0
    jacobsthal = np.zeros((25, 25), dtype=np.int64)
    for left_item in range(25):
        for right_item in range(25):
            diff_real = (left_item % 5 - right_item % 5) % 5
            diff_root = (left_item // 5 - right_item // 5) % 5
            jacobsthal[left_item, right_item] = character[diff_real + 5 * diff_root]
    conference = np.zeros((26, 26), dtype=np.int64)
    conference[0, 1:] = 1
    conference[1:, 0] = 1
    conference[1:, 1:] = jacobsthal
    outer_part = np.array([[1, -1], [-1, -1]], dtype=np.int64)
    inner_part = np.array([[1, 1], [1, -1]], dtype=np.int64)
    return np.kron(conference, outer_part) + np.kron(np.eye(26, dtype=np.int64), inner_part)


def sylvester_static(order_size):
    position = np.arange(order_size)
    parity = np.zeros((order_size, order_size), dtype=np.int64)
    for bit_place in range(max(order_size.bit_length() - 1, 0)):
        parity = parity + (position[:, None] >> bit_place & position[None, :] >> bit_place & 1)
    return 1 - 2 * (parity & 1)


def inner_table():
    table = np.kron(paley_table(), sylvester_static(BLK))
    order = (4 * np.arange(416)[None, :] + np.arange(4)[:, None]).reshape(-1)
    return table[:, order].astype(np.float32)


def remote(src, dst, send_sem, recv_sem, device):
    return pltpu.make_async_remote_copy(
        src_ref=src, dst_ref=dst, send_sem=send_sem, recv_sem=recv_sem, device_id=device, device_id_type=MESH
    )


def place():
    dp = lax.axis_index("dp")
    t = lax.axis_index("tensor")
    x, yh = lax.div(dp, 2), lax.rem(dp, 2)
    yl, z, core = lax.div(t, 16), lax.rem(lax.div(t, 2), 8), lax.rem(t, 2)
    return dp, t, x, yh, yl, z, core


def enter(devices):
    barrier = pltpu.get_barrier_semaphore()
    for device in devices:
        pl.semaphore_signal(barrier, inc=1, device_id=device, device_id_type=MESH)
    pl.semaphore_wait(barrier, len(devices))


def unpack(words, scale, j):
    levels = (words & (7 << (3 * j))).astype(F32).astype(BF16) - jnp.asarray(4.0 * 8.0**j, BF16)
    return levels * (scale * 8.0**-j).astype(BF16)


CH = 13


def gate_up_kernel(
    tok, gcodes, ucodes, gs, us, flip, out,
    gbuf, ubuf, w, xg, pb, r1, r2, s3, r3, own,
    ld, ys, yr, ps, pr, ss, sr, cs, cr, r1s, r1r, r2s, r2r, r3s, r3r,
):
    dp, t, x, yh, yl, z, core = place()
    yo = 1 - yl
    sign = 1 - 2 * core
    tid = lambda a, b, c: a * 16 + b * 2 + c
    zat = lambda k: lax.rem(z + sign * k + 8, 8)
    dev_y = (dp, tid(yo, z, core))
    dev_c = (dp, tid(yl, z, 1 - core))
    dev_p = (dp, tid(yl, zat(1), core))
    dev_s = (dp, tid(yl, zat(-1), core))
    xr, xl, x2 = lax.rem(x + 1, 4), lax.rem(x + 3, 4), lax.rem(x + 2, 4)
    dev_r = (xr * 2 + yh, t)
    dev_l = (xl * 2 + yh, t)
    dev_h = (x * 2 + 1 - yh, t)

    loads = [pltpu.make_async_copy(gcodes, gbuf, ld.at[0]), pltpu.make_async_copy(ucodes, ubuf, ld.at[1])]
    for copy in loads:
        copy.start()

    rows_i = lax.broadcasted_iota(jnp.int32, (512, 512), 0)
    cols_i = lax.broadcasted_iota(jnp.int32, (512, 512), 1)
    pick = jnp.where(rows_i == 4 * (cols_i % 128) + cols_i // 128, 1.0, 0.0).astype(BF16)
    for q in range(4):
        cols = slice(512 * q, 512 * q + 512)
        xg[yl, z, core, :, cols] = jnp.dot(tok[:, cols], pick, preferred_element_type=F32).astype(BF16)

    enter([dev_y, dev_c, dev_p, dev_s, dev_r, dev_l, dev_h])

    yv = (yl, yo)

    def copy_y(y):
        return remote(xg.at[y, z, core], xg.at[y, z, core], ys.at[0], yr.at[0], dev_y)

    def copy_p(k, yy, away):
        block = xg.at[yv[yy], zat(-away), core]
        return remote(block, block, ps.at[k - 1, yy], pr.at[k - 1, yy], dev_p)

    def copy_s(k, yy, away):
        block = xg.at[yv[yy], zat(away), core]
        return remote(block, block, ss.at[k - 1, yy], sr.at[k - 1, yy], dev_s)

    def copy_c(slot, yy, back, c):
        block = xg.at[yv[yy], zat(back), c]
        return remote(block, block, cs.at[slot, yy], cr.at[slot, yy], dev_c)

    def dequant(c, carry):
        cols = pl.ds(pl.multiple_of(128 * c, 128), 128)
        for side, (buf, sc) in enumerate(((gbuf, gs), (ubuf, us))):
            for g in range(16):
                words = buf[32 * g : 32 * g + 32, cols]
                scale = sc[g : g + 1, cols]
                for j in range(4):
                    row = 512 * (g // 4) + 128 * j + 32 * (g % 4)
                    w[c, row : row + 32, 128 * side : 128 * side + 128] = unpack(words, scale, j)
        return carry

    sends = []

    def go(copy):
        copy.start()
        sends.append(copy)

    go(copy_y(yl))
    go(copy_p(1, 0, 0))
    go(copy_s(1, 0, 0))
    go(copy_c(0, 0, 0, core))
    for copy in loads:
        copy.wait()
    lax.fori_loop(0, 1, dequant, 0)
    copy_y(yo).wait_recv()
    go(copy_p(1, 1, 0))
    go(copy_s(1, 1, 0))
    go(copy_c(0, 1, 0, core))
    spans = {1: (1, 4), 2: (4, 7), 3: (7, 10), 4: (10, 13)}
    for k in range(1, 5):
        for yy in range(2):
            copy_p(k, yy, k).wait_recv()
            if k < 4:
                go(copy_p(k + 1, yy, k))
            go(copy_c(k, yy, -k, core))
            if k < 4:
                copy_s(k, yy, k).wait_recv()
                if k < 3:
                    go(copy_s(k + 1, yy, k))
                go(copy_c(4 + k, yy, k, core))
        lax.fori_loop(*spans[k], dequant, 0)
    for slot in range(8):
        back = slot if slot < 5 else -(slot - 4)
        for yy in range(2):
            copy_c(slot, yy, back, 1 - core).wait_recv()

    def first(c):
        far_a = pb.at[c, pl.ds(pl.multiple_of(128 * x2, 64), 64)]
        far_b = pb.at[c, pl.ds(pl.multiple_of(128 * x2 + 64, 64), 64)]
        return (
            remote(far_a, r1.at[0, c], r1s.at[0, c], r1r.at[0, c], dev_r),
            remote(far_b, r1.at[1, c], r1s.at[1, c], r1r.at[1, c], dev_l),
        )

    def second(c):
        near_r = pb.at[c, pl.ds(pl.multiple_of(128 * xr, 128), 128)]
        near_l = pb.at[c, pl.ds(pl.multiple_of(128 * xl, 128), 128)]
        return (
            remote(near_r, r2.at[0, c], r2s.at[0, c], r2r.at[0, c], dev_r),
            remote(near_l, r2.at[1, c], r2s.at[1, c], r2r.at[1, c], dev_l),
        )

    def third(c):
        return remote(s3.at[c], r3.at[c], r3s.at[c], r3r.at[c], dev_h)

    def multiply(c, carry):
        both = jnp.dot(xg[...].reshape(512, 2048), w[c], preferred_element_type=F32)
        pb[c] = both.astype(BF16)
        for copy in first(c):
            copy.start()
        return carry

    def round_two(c, carry):
        arrive, leave = first(c), second(c)
        arrive[0].wait_recv()
        rows = pl.ds(pl.multiple_of(128 * xr, 64), 64)
        pb[c, rows] = (pb[c, rows].astype(F32) + r1[0, c].astype(F32)).astype(BF16)
        leave[0].start()
        arrive[1].wait_recv()
        rows = pl.ds(pl.multiple_of(128 * xl + 64, 64), 64)
        pb[c, rows] = (pb[c, rows].astype(F32) + r1[1, c].astype(F32)).astype(BF16)
        leave[1].start()
        return carry

    def round_three(c, carry):
        arrive = second(c)
        arrive[0].wait_recv()
        arrive[1].wait_recv()

        def total(half):
            here = pl.ds(pl.multiple_of(128 * x + 64 * half, 64), 64)
            there = pl.ds(pl.multiple_of(64 * half, 64), 64)
            return pb[c, here].astype(F32) + r2[0, c, there].astype(F32) + r2[1, c, there].astype(F32)

        s3[c] = total(1 - yh).astype(BF16)
        third(c).start()
        own[c] = total(yh)
        return carry

    def finish(c, carry):
        third(c).wait_recv()
        full = own[c] + r3[c].astype(F32)
        gate, up = full[:, :128], full[:, 128:]
        cols = pl.ds(pl.multiple_of(128 * c, 128), 128)
        hidden = (gate / (1.0 + jnp.exp(-gate)) * up).astype(BF16).astype(F32)
        out[:, cols] = jnp.where(flip[:, cols] == 1, hidden, -hidden).astype(BF16)
        return carry

    def drain(c, carry):
        for copy in first(c) + second(c) + (third(c),):
            copy.wait_send()
        return carry

    for step in (multiply, round_two, round_three, finish, drain):
        lax.fori_loop(0, CH, step, 0)
    for copy in sends:
        copy.wait_send()


def gate_up(tokens, gate_codes, gate_scales, up_codes, up_scales, flip_signs):
    vm = pl.BlockSpec(memory_space=pltpu.VMEM)
    hbm = pl.BlockSpec(memory_space=pl.ANY)
    dma = pltpu.SemaphoreType.DMA
    return pl.pallas_call(
        gate_up_kernel,
        out_shape=jax.ShapeDtypeStruct((64, 1664), BF16),
        in_specs=[vm, hbm, hbm, vm, vm, vm],
        out_specs=vm,
        scratch_shapes=[
            pltpu.VMEM((512, 1664), jnp.int32),
            pltpu.VMEM((512, 1664), jnp.int32),
            pltpu.VMEM((CH, 2048, 256), BF16),
            pltpu.VMEM((2, 8, 2, 16, 2048), BF16),
            pltpu.VMEM((CH, 512, 256), BF16),
            pltpu.VMEM((2, CH, 64, 256), BF16),
            pltpu.VMEM((2, CH, 128, 256), BF16),
            pltpu.VMEM((CH, 64, 256), BF16),
            pltpu.VMEM((CH, 64, 256), BF16),
            pltpu.VMEM((CH, 64, 256), F32),
            dma((2,)), dma((1,)), dma((1,)),
            dma((4, 2)), dma((4, 2)), dma((3, 2)), dma((3, 2)), dma((8, 2)), dma((8, 2)),
            dma((2, CH)), dma((2, CH)), dma((2, CH)), dma((2, CH)), dma((CH,)), dma((CH,)),
        ],
        compiler_params=pltpu.CompilerParams(
            collective_id=0, has_side_effects=True, vmem_limit_bytes=VMEM_LIMIT
        ),
        cost_estimate=pl.CostEstimate(flops=7 * 10**9, bytes_accessed=10**7, transcendentals=10**5),
    )(tokens, gate_codes, up_codes, gate_scales.astype(F32), up_scales.astype(F32), flip_signs[None, :])


HAND = 26


def rotate_kernel(hid, table_hbm, out, table, gin, gout, hm, ld, as_, ar, bs, br):
    dp, t, x, yh, yl, z, core = place()
    load = pltpu.make_async_copy(table_hbm, table, ld.at[0])
    load.start()
    others = [lax.rem(t + k, 32) for k in range(1, 32)]
    enter([(dp, o) for o in others])

    def tile(ref, o):
        return ref.at[pl.ds(pl.multiple_of(32 * lax.rem(o, 2), 32), 32), pl.ds(pl.multiple_of(128 * lax.div(o, 2), 128), 128)]

    def ahead(o):
        return remote(tile(hid, o), gin.at[t], as_.at[o], ar.at[t], (dp, o))

    def back(o):
        return remote(gout.at[o], tile(hm, t), bs.at[o], br.at[t], (dp, o))

    def send_ahead(k, carry):
        o = lax.rem(t + k, 32)

        @pl.when(o < HAND)
        def _():
            ahead(o).start()

        return carry

    lax.fori_loop(1, 32, send_ahead, 0)

    @pl.when(t < HAND)
    def _():
        gin[t] = tile(hid, t)[...]

        def arrive(k, carry):
            o = lax.rem(t + k, 32)
            remote(gin.at[o], gin.at[o], as_.at[o], ar.at[o], (dp, o)).wait_recv()
            return carry

        lax.fori_loop(1, 32, arrive, 0)
        for half in range(2):
            rows = slice(16 * half, 16 * half + 16)
            values = [gin[g, rows].astype(F32) for g in range(32)]
            for bit in range(5):
                step = 1 << bit
                values = [
                    values[g] + values[g + step] if g & step == 0 else values[g - step] - values[g]
                    for g in range(32)
                ]
            for g in range(32):
                gout[g, rows] = values[g].astype(BF16)

        def send_back(k, carry):
            back(lax.rem(t + k, 32)).start()
            return carry

        lax.fori_loop(1, 32, send_back, 0)
        tile(hm, t)[...] = gout[t]

    def arrive_back(k, carry):
        o = lax.rem(t + k, 32)

        @pl.when(o < HAND)
        def _():
            remote(gout.at[o], tile(hm, o), bs.at[o], br.at[o], (dp, o)).wait_recv()

        return carry

    lax.fori_loop(1, 32, arrive_back, 0)
    load.wait()
    out[...] = (jnp.dot(hm[...], table[...], preferred_element_type=F32) * FF**-0.5).astype(BF16)

    def drain(k, carry):
        o = lax.rem(t + k, 32)

        @pl.when(o < HAND)
        def _():
            ahead(o).wait_send()

        @pl.when(t < HAND)
        def _():
            back(o).wait_send()

        return carry

    lax.fori_loop(1, 32, drain, 0)


def rotate(hidden):
    vm = pl.BlockSpec(memory_space=pltpu.VMEM)
    hbm = pl.BlockSpec(memory_space=pl.ANY)
    dma = pltpu.SemaphoreType.DMA
    return pl.pallas_call(
        rotate_kernel,
        out_shape=jax.ShapeDtypeStruct((64, 1664), BF16),
        in_specs=[vm, hbm],
        out_specs=vm,
        scratch_shapes=[
            pltpu.VMEM((1664, 1664), BF16),
            pltpu.VMEM((32, 32, 128), BF16),
            pltpu.VMEM((32, 32, 128), BF16),
            pltpu.VMEM((64, 1664), BF16),
            dma((1,)), dma((32,)), dma((32,)), dma((32,)), dma((32,)),
        ],
        compiler_params=pltpu.CompilerParams(
            collective_id=1, has_side_effects=True, vmem_limit_bytes=VMEM_LIMIT
        ),
        cost_estimate=pl.CostEstimate(flops=4 * 10**8, bytes_accessed=6 * 10**6, transcendentals=0),
    )(hidden, jnp.asarray(inner_table(), dtype=BF16))


NC = 4
WC = 512


def down_kernel(
    rot, dcodes, ds_, out,
    dbuf, w, rg, pb, rc, rz1, rz, tot, ry,
    ld, ags, agr, ccs, ccr, zs, zr, yys, yyr,
):
    dp, t, x, yh, yl, z, core = place()
    ho, yo = 1 - yh, 1 - yl
    xr, xl, x2 = lax.rem(x + 1, 4), lax.rem(x + 3, 4), lax.rem(x + 2, 4)
    tid = lambda a, b, c: a * 16 + b * 2 + c
    zat = lambda k: lax.rem(z + k + 8, 8)
    dev_r, dev_l, dev_h = (xr * 2 + yh, t), (xl * 2 + yh, t), (x * 2 + ho, t)
    dev_y, dev_c = (dp, tid(yo, z, core)), (dp, tid(yl, z, 1 - core))
    dev_u, dev_d = (dp, tid(yl, zat(1), core)), (dp, tid(yl, zat(-1), core))

    load = pltpu.make_async_copy(dcodes, dbuf, ld.at[0])
    load.start()
    rg[dp] = rot[...]
    enter([dev_r, dev_l, dev_h, dev_y, dev_c, dev_u, dev_d])

    def block(kind, dev, slot):
        b = rg.at[kind]
        return remote(b, b, ags.at[slot], agr.at[slot], dev)

    mine, mate = x * 2 + yh, x * 2 + ho
    sends = [block(mine, dev_h, 0), block(mine, dev_r, 1), block(mine, dev_l, 2)]
    for copy in sends:
        copy.start()

    load.wait()

    def dequant(c, carry):
        cols = pl.ds(pl.multiple_of(128 * c, 128), 128)
        for g in range(13):
            words = dbuf[32 * g : 32 * g + 32, cols]
            scale = ds_[g : g + 1, cols]
            for j in range(4):
                row = 416 * j + 32 * g
                w[row : row + 32, cols] = unpack(words, scale, j)
        return carry

    lax.fori_loop(0, 4, dequant, 0)
    block(mate, dev_h, 0).wait_recv()
    more = [block(mate, dev_r, 3), block(mate, dev_l, 4)]
    for copy in more:
        copy.start()
    block(xl * 2 + yh, dev_r, 1).wait_recv()
    more.append(block(xl * 2 + yh, dev_r, 5))
    more[-1].start()
    lax.fori_loop(4, 10, dequant, 0)
    block(xr * 2 + ho, dev_l, 4).wait_recv()
    more.append(block(xr * 2 + ho, dev_l, 6))
    more[-1].start()
    lax.fori_loop(10, 16, dequant, 0)
    block(xr * 2 + yh, dev_l, 2).wait_recv()
    block(xl * 2 + ho, dev_r, 3).wait_recv()
    block(x2 * 2 + yh, dev_r, 5).wait_recv()
    block(x2 * 2 + ho, dev_l, 6).wait_recv()

    def pair(c):
        return remote(pb.at[c, 1 - core], rc.at[c], ccs.at[c], ccr.at[c], dev_c)

    def one(c):
        return (
            remote(pb.at[c, core, 0, zat(4)], rz1.at[0, c], zs.at[0, 0, c], zr.at[0, 0, c], dev_u),
            remote(pb.at[c, core, 1, zat(4)], rz1.at[1, c], zs.at[1, 0, c], zr.at[1, 0, c], dev_d),
        )

    def ring(r, c):
        k = 5 - r
        return (
            remote(pb.at[c, core, :, zat(k)], rz.at[0, r - 2, c], zs.at[0, r - 1, c], zr.at[0, r - 1, c], dev_u),
            remote(pb.at[c, core, :, zat(-k)], rz.at[1, r - 2, c], zs.at[1, r - 1, c], zr.at[1, r - 1, c], dev_d),
        )

    def across(c):
        return remote(tot.at[c, yo], ry.at[c], yys.at[c], yyr.at[c], dev_y)

    def multiply(c, carry):
        for part in range(2):
            cols = pl.ds(pl.multiple_of(WC * c + 256 * part, 256), 256)
            terms = jnp.dot(rg[...].reshape(512, 1664), w[:, cols], preferred_element_type=F32).astype(BF16)
            for cc in range(2):
                for yy in range(2):
                    for zz in range(8):
                        row = 16 * (16 * yy + 2 * zz + cc)
                        pb[c, cc, yy, zz, :, 256 * part : 256 * part + 256] = terms[row : row + 16]
        pair(c).start()
        return carry

    def round_one(c, carry):
        pair(c).wait_recv()
        pb[c, core] = (pb[c, core].astype(F32) + rc[c].astype(F32)).astype(BF16)
        for copy in one(c):
            copy.start()
        return carry

    def round_two(c, carry):
        for side in range(2):
            one(c)[side].wait_recv()
            at = zat(3 - 6 * side)
            pb[c, core, side, at] = (pb[c, core, side, at].astype(F32) + rz1[side, c].astype(F32)).astype(BF16)
            ring(2, c)[side].start()
        return carry

    def round_more(r, c, carry):
        for side in range(2):
            ring(r - 1, c)[side].wait_recv()
            at = zat((5 - r) * (1 - 2 * side))
            for yy in range(2):
                pb[c, core, yy, at] = (
                    pb[c, core, yy, at].astype(F32) + rz[side, r - 3, c, yy].astype(F32)
                ).astype(BF16)
            ring(r, c)[side].start()
        return carry

    def round_last(c, carry):
        for side in range(2):
            ring(4, c)[side].wait_recv()
        for yy in range(2):
            tot[c, yy] = (
                pb[c, core, yy, z].astype(F32) + rz[0, 2, c, yy].astype(F32) + rz[1, 2, c, yy].astype(F32)
            ).astype(BF16)
        across(c).start()
        return carry

    def finish(c, carry):
        across(c).wait_recv()
        cols = pl.ds(pl.multiple_of(WC * c, WC), WC)
        out[:, cols] = (tot[c, yl].astype(F32) + ry[c].astype(F32)).astype(BF16)
        return carry

    def drain(c, carry):
        for copy in (pair(c),) + one(c) + ring(2, c) + ring(3, c) + ring(4, c) + (across(c),):
            copy.wait_send()
        return carry

    steps = (
        multiply, round_one, round_two,
        functools.partial(round_more, 3), functools.partial(round_more, 4),
        round_last, finish, drain,
    )
    for step in steps:
        lax.fori_loop(0, NC, step, 0)
    for copy in sends + more:
        copy.wait_send()


def down(rotated, down_codes, down_scales):
    vm = pl.BlockSpec(memory_space=pltpu.VMEM)
    hbm = pl.BlockSpec(memory_space=pl.ANY)
    dma = pltpu.SemaphoreType.DMA
    return pl.pallas_call(
        down_kernel,
        out_shape=jax.ShapeDtypeStruct((16, 2048), BF16),
        in_specs=[vm, hbm, vm],
        out_specs=vm,
        scratch_shapes=[
            pltpu.VMEM((416, 2048), jnp.int32),
            pltpu.VMEM((1664, 2048), BF16),
            pltpu.VMEM((8, 64, 1664), BF16),
            pltpu.VMEM((NC, 2, 2, 8, 16, WC), BF16),
            pltpu.VMEM((NC, 2, 8, 16, WC), BF16),
            pltpu.VMEM((2, NC, 16, WC), BF16),
            pltpu.VMEM((2, 3, NC, 2, 16, WC), BF16),
            pltpu.VMEM((NC, 2, 16, WC), BF16),
            pltpu.VMEM((NC, 16, WC), BF16),
            dma((1,)), dma((7,)), dma((7,)), dma((NC,)), dma((NC,)),
            dma((2, 4, NC)), dma((2, 4, NC)), dma((NC,)), dma((NC,)),
        ],
        compiler_params=pltpu.CompilerParams(
            collective_id=2, has_side_effects=True, vmem_limit_bytes=VMEM_LIMIT
        ),
        cost_estimate=pl.CostEstimate(flops=4 * 10**9, bytes_accessed=4 * 10**6, transcendentals=0),
    )(rotated, down_codes, down_scales.astype(F32))


def per_device(
    tokens, gate_codes, gate_scales, up_codes, up_scales, down_codes, down_scales, flip_signs
):
    hidden = gate_up(tokens, gate_codes, gate_scales, up_codes, up_scales, flip_signs)
    return down(rotate(hidden), down_codes, down_scales)


def solution(mesh):
    return jax.shard_map(
        per_device,
        mesh=mesh,
        in_specs=(
            P("tensor", "dp"),
            P("dp", "tensor"),
            P("dp", "tensor"),
            P("dp", "tensor"),
            P("dp", "tensor"),
            P("tensor", "dp"),
            P("tensor", "dp"),
            P("tensor"),
        ),
        out_specs=P("tensor", "dp"),
        check_vma=False,
    )
```

time: 418 us -> 145 us (0.35)
  waiting for transfers between devices: 259 us -> 0 us
  Pallas kernels: 0 us -> 138 us
  local copies, waits for them, and re-layouts: 81.1 us -> 2.77 us
  matrix products: 25.4 us -> 0 us
  other arithmetic: 26.8 us -> 3.57 us
  between operations: 13.3 us -> 0.04 us
  starting transfers between devices: 11.1 us -> 0 us
    pallas_call x0 -> x3, Pallas kernels: none -> 138 us  [the longest x1 65.1 us: gate_up(): pl.pallas_call(gate_up_kernel, out_shape=jax.ShapeDtypeStruct((64, 1664),...]
    reduce_scatter x1 -> x0, waiting for transfers between devices: 118 us -> none  [per_device(): lax.psum_scatter(terms.astype(jnp.bfloat16), 'tensor', scatter_dimension=...]
    unnamed x5 -> x0, waiting for transfers between devices: 86.8 us -> none
    shift_right_arithmetic x10 -> x0, local copies, waits for them, and re-layouts: 75.9 us -> none  [dequant(): jnp.right_shift(code_words[:, None, :], shifts[None, :, None])]
    ppermute x5 -> x0, waiting for transfers between devices: 30.5 us -> none  [from_partner(): lax.ppermute(value, axis, [(i, i ^ 1 << bit) for i in range(lax.axis_size...]
    dot_general x3 -> x0, matrix products: 25.4 us -> none  [the longest x1 12.8 us: per_device(): jnp.dot(all_rows, both_weights, preferred_element_type=jnp.float32)]
    all_gather x2 -> x0, waiting for transfers between devices: 23.6 us -> none  [the longest x1 19.2 us: per_device(): lax.all_gather(rotated, 'dp', axis=0, tiled=True)]
    convert_element_type x11 -> x3, other arithmetic: 26.8 us -> 3.57 us  [the longest x1 1.46 us: gate_up(): up_scales.astype(F32)]
  transfers between devices with their start and end apart: 9 -> 0, of which waited for: 9 -> 0; matrix products, arithmetic and copies ran while one was open for 24% -> 0% of each run, Pallas kernels for 0% -> 0%
where the time goes in v1:
time: 145 us; the launch traced here: 144 us
  Pallas kernels  138 us (95%)
  other arithmetic  3.57 us (2%)
  local copies, waits for them, and re-layouts  2.77 us (2%)
    pallas_call x1, Pallas kernels, gate_up(): pl.pallas_call(gate_up_kernel, out_shape=jax.ShapeDtypeStruct((64, 1664),...  65.1 us
    pallas_call x1, Pallas kernels, down(): pl.pallas_call(down_kernel, out_shape=jax.ShapeDtypeStruct((16, 2048), BF...  48.3 us
    pallas_call x1, Pallas kernels, rotate(): pl.pallas_call(rotate_kernel, out_shape=jax.ShapeDtypeStruct((64, 1664),...  24.6 us

profile of v1, /device:TPU:2, one launch (start us, length us, event | category | flops | bytes accessed | tf_op | source)
XLA Modules:
  0.0 144.4 jit_solution(6208334434716818613)
XLA Ops:
  0.0 1.3 broadcast_in_dim.3.flip
  1.3 1.4 %convert_element_type.9.gs = f32[16,1664]{1,0:T(8,128)} convert(bf16[16,1664]{1,0:T(8,128)(2,1)} %param.11) | non-fusion elementwise | flops 26624 | bytes 159744 | tf_op jit(solution)/shard_map/convert_element_type | solution.py:285
  2.7 1.5 %convert_element_type.10.us = f32[16,1664]{1,0:T(8,128)} convert(bf16[16,1664]{1,0:T(8,128)(2,1)} %param.13) | non-fusion elementwise | flops 26624 | bytes 159744 | tf_op jit(solution)/shard_map/convert_element_type | solution.py:285
  4.2 65.1 %shard_map.91.hid = bf16[64,1664]{1,0:T(8,128)(2,1)} custom-call(bf16[16,2048]{1,0:T(8,128)(2,1)} %tok.1, s32[512,1664]{1,0:T(8,128)} %gcodes.1, s32[512,1664]{1,0:T(8,128)} %ucodes.1, f32[16,1664]{1,0:T(8,128)} %convert_element_type.9.gs, f32[16,1664]{1,0:T(8,128)} %convert_element_type.10.us, s32[1,1664]{1,0:T(1,128)} %broadcast_in_dim.3.flip), custom_call_target="tpu_custom_call" | custom-call | flops 7000000000 | bytes 10000000 | tf_op jit(solution)/shard_map/pallas_call | solution.py:261
  69.3 0.0 copy-start
  69.4 24.6 %shard_map.92.rot = bf16[64,1664]{1,0:T(8,128)(2,1)} custom-call(bf16[64,1664]{1,0:T(8,128)(2,1)} %shard_map.91.hid, bf16[1664,1664]{1,0:T(8,128)(2,1)} %constant.2.clone.table_hbm), custom_call_target="tpu_custom_call" | custom-call | flops 400000000 | bytes 6000000 | tf_op jit(solution)/shard_map/pallas_call | solution.py:380
  93.9 0.0 copy-done
  93.9 0.7 convert_element_type.11.ds_
  94.6 48.3 %shard_map.93 = bf16[16,2048]{1,0:T(8,128)(2,1)} custom-call(bf16[64,1664]{1,0:T(8,128)(2,1)} %shard_map.92.rot, s32[416,2048]{1,0:T(8,128)} %dcodes.1, f32[13,2048]{1,0:T(8,128)} %convert_element_type.11.ds_), custom_call_target="tpu_custom_call" | custom-call | flops 4000000000 | bytes 4000000 | tf_op jit(solution)/shard_map/pallas_call | solution.py:554
  142.9 1.5 %copy.11 = bf16[16,2048]{1,0:T(8,128)(2,1)} copy(bf16[16,2048]{1,0:T(8,128)(2,1)} %shard_map.93) | data formatting | bytes 131072
Async XLA Ops:
  69.3 24.6 %copy-start = (bf16[13,2048]{1,0:T(8,128)(2,1)S(1)}, bf16[13,2048]{1,0:T(8,128)(2,1)}, u32[]{:S(2)}) copy-start(bf16[13,2048]{1,0:T(8,128)(2,1)} %param.15) | copy-start | bytes 159748

commit v2 on v0

v2 whole, which is shorter than its diff:
```python
import functools

import jax
import jax.numpy as jnp
import numpy as np
from jax import lax
from jax.experimental import pallas as pl
from jax.experimental.pallas import tpu as pltpu
from jax.sharding import PartitionSpec as P

FF = 53248
KB = 52
BLK = 32
MESH = pl.DeviceIdType.MESH
BF16 = jnp.bfloat16
F32 = jnp.float32
VMEM_LIMIT = 60 * 1024 * 1024


def paley_table():
    field_square = np.zeros(25, dtype=np.int64)
    for first_part in range(5):
        for second_part in range(5):
            if first_part == 0 and second_part == 0:
                continue
            real_part = (first_part * first_part + 2 * second_part * second_part) % 5
            root_part = 2 * first_part * second_part % 5
            field_square[real_part + 5 * root_part] = 1
    character = np.where(field_square == 1, 1, -1)
    character[0] = 0
    jacobsthal = np.zeros((25, 25), dtype=np.int64)
    for left_item in range(25):
        for right_item in range(25):
            diff_real = (left_item % 5 - right_item % 5) % 5
            diff_root = (left_item // 5 - right_item // 5) % 5
            jacobsthal[left_item, right_item] = character[diff_real + 5 * diff_root]
    conference = np.zeros((26, 26), dtype=np.int64)
    conference[0, 1:] = 1
    conference[1:, 0] = 1
    conference[1:, 1:] = jacobsthal
    outer_part = np.array([[1, -1], [-1, -1]], dtype=np.int64)
    inner_part = np.array([[1, 1], [1, -1]], dtype=np.int64)
    return np.kron(conference, outer_part) + np.kron(np.eye(26, dtype=np.int64), inner_part)


def sylvester_static(order_size):
    position = np.arange(order_size)
    parity = np.zeros((order_size, order_size), dtype=np.int64)
    for bit_place in range(max(order_size.bit_length() - 1, 0)):
        parity = parity + (position[:, None] >> bit_place & position[None, :] >> bit_place & 1)
    return 1 - 2 * (parity & 1)


def inner_table():
    table = np.kron(paley_table(), sylvester_static(BLK))
    order = (4 * np.arange(416)[None, :] + np.arange(4)[:, None]).reshape(-1)
    return table[:, order].astype(np.float32)


def remote(src, dst, send_sem, recv_sem, device):
    return pltpu.make_async_remote_copy(
        src_ref=src, dst_ref=dst, send_sem=send_sem, recv_sem=recv_sem, device_id=device, device_id_type=MESH
    )


def place():
    dp = lax.axis_index("dp")
    t = lax.axis_index("tensor")
    x, yh = lax.div(dp, 2), lax.rem(dp, 2)
    yl, z, core = lax.div(t, 16), lax.rem(lax.div(t, 2), 8), lax.rem(t, 2)
    return dp, t, x, yh, yl, z, core


def unpack(words, scale, j):
    levels = (words & (7 << (3 * j))).astype(F32).astype(BF16) - jnp.asarray(4.0 * 8.0**j, BF16)
    return levels * (scale * 8.0**-j).astype(BF16)


CH = 13
GROUPS = ((0, 4, True, True), (4, 3, True, True), (7, 3, True, True), (10, 3, False, False))
ORDER = (0, 1, 3, 2)
NC = 4
WC = 512


def kernel(
    tok, gcodes, ucodes, dcodes, gs, us, ds_, flip, table_hbm, out,
    cbuf, ubuf, w, xg, pb, r1, r2, ry, s3, r3, own,
    table, hid, gin, gout, rg, acc, wd, rot,
    qb, rc, rz1, rz, tot, rl,
    ld, ys, yr, ps, pr, ss, sr, cs, cr, as_, ar, bs, br, r1s, r1r, r2s, r2r, r3s, r3r, ags, agr,
    ccs, ccr, zs, zr, yys, yyr,
):
    dp, t, x, yh, yl, z, core = place()
    ho, yo, co = 1 - yh, 1 - yl, 1 - core
    sign = 1 - 2 * core
    tid = lambda a, b, c: a * 16 + b * 2 + c
    zat = lambda k: lax.rem(z + k + 8, 8)
    zsg = lambda k: lax.rem(z + sign * k + 8, 8)
    xr, xl, x2 = lax.rem(x + 1, 4), lax.rem(x + 3, 4), lax.rem(x + 2, 4)
    dev_y, dev_c = (dp, tid(yo, z, core)), (dp, tid(yl, z, co))
    dev_p, dev_s = (dp, tid(yl, zsg(1), core)), (dp, tid(yl, zsg(-1), core))
    dev_u, dev_d = (dp, tid(yl, zat(1), core)), (dp, tid(yl, zat(-1), core))
    dev_r, dev_l, dev_h = (xr * 2 + yh, t), (xl * 2 + yh, t), (x * 2 + ho, t)

    gbuf, dbuf = cbuf.at[:, pl.ds(0, 1664)], cbuf.at[pl.ds(0, 416)]
    load_g = pltpu.make_async_copy(gcodes, gbuf, ld.at[0])
    load_u = pltpu.make_async_copy(ucodes, ubuf, ld.at[1])
    load_t = pltpu.make_async_copy(table_hbm, table, ld.at[2])
    load_d = pltpu.make_async_copy(dcodes, dbuf, ld.at[3])
    load_g.start()
    load_u.start()

    rows_i = lax.broadcasted_iota(jnp.int32, (512, 512), 0)
    cols_i = lax.broadcasted_iota(jnp.int32, (512, 512), 1)
    pick = jnp.where(rows_i == 4 * (cols_i % 128) + cols_i // 128, 1.0, 0.0).astype(BF16)
    for q in range(4):
        cols = slice(512 * q, 512 * q + 512)
        xg[yl, z, core, :, cols] = jnp.dot(tok[:, cols], pick, preferred_element_type=F32).astype(BF16)

    barrier = pltpu.get_barrier_semaphore()
    for device in (dev_r, dev_l, dev_h):
        pl.semaphore_signal(barrier, inc=1, device_id=device, device_id_type=MESH)

    def greet(k, carry):
        pl.semaphore_signal(barrier, inc=1, device_id=(dp, lax.rem(t + k, 32)), device_id_type=MESH)
        return carry

    lax.fori_loop(1, 32, greet, 0)
    pl.semaphore_wait(barrier, 34)

    sends = []

    def go(copy):
        copy.start()
        sends.append(copy)

    yv = (yl, yo)

    def piece(y, back, c, h):
        return xg.at[y, zsg(back), c, :, pl.ds(1024 * h, 1024)]

    def copy_y(y, back, slot, h):
        block = piece(y, back, core, h)
        return remote(block, block, ys.at[slot, h], yr.at[slot, h], dev_y)

    def copy_p(k, yy, away, h):
        block = piece(yv[yy], -away, core, h)
        return remote(block, block, ps.at[k - 1, yy, h], pr.at[k - 1, yy, h], dev_p)

    def copy_s(k, yy, away, h):
        block = piece(yv[yy], away, core, h)
        return remote(block, block, ss.at[k - 1, yy, h], sr.at[k - 1, yy, h], dev_s)

    def copy_c(slot, yy, back, c, h):
        block = piece(yv[yy], back, c, h)
        return remote(block, block, cs.at[slot, yy, h], cr.at[slot, yy, h], dev_c)

    def dequant(c, carry):
        cols = pl.ds(pl.multiple_of(128 * c, 128), 128)
        for side, (buf, sc) in enumerate(((gbuf, gs), (ubuf, us))):
            scales = sc[:, cols].astype(F32)
            for g in range(16):
                words = buf[32 * g : 32 * g + 32, cols]
                for j in range(4):
                    row = 512 * (g // 4) + 128 * j + 32 * (g % 4)
                    w[c, row : row + 32, 128 * side : 128 * side + 128] = unpack(words, scales[g : g + 1], j)
        return carry

    def forward(k, yy, last_p, last_s):
        for h in range(2):
            copy_p(k, yy, k, h).wait_recv()
            if k < last_p:
                go(copy_p(k + 1, yy, k, h))
            if yy == 0 and k >= 3:
                go(copy_y(yl, -k, k - 2, h))
            go(copy_c(k, yy, -k, core, h))
            if k <= last_s:
                copy_s(k, yy, k, h).wait_recv()
                if k < last_s:
                    go(copy_s(k + 1, yy, k, h))
                if yy == 0 and k >= 3:
                    go(copy_y(yl, k, 3, h))
                go(copy_c(4 + k, yy, k, core, h))

    for h in range(2):
        go(copy_p(1, 0, 0, h))
        go(copy_s(1, 0, 0, h))
        go(copy_y(yl, 0, 0, h))
    for h in range(2):
        go(copy_c(0, 0, 0, core, h))
    load_g.wait()
    load_u.wait()
    lax.fori_loop(0, 3, dequant, 0)
    forward(1, 0, 4, 3)
    for h in range(2):
        copy_y(yo, 0, 0, h).wait_recv()
        go(copy_p(1, 1, 0, h))
        go(copy_s(1, 1, 0, h))
        go(copy_c(0, 1, 0, core, h))
    lax.fori_loop(3, 6, dequant, 0)
    forward(2, 0, 4, 3)
    lax.fori_loop(6, 8, dequant, 0)
    forward(1, 1, 2, 2)
    lax.fori_loop(8, 10, dequant, 0)
    forward(3, 0, 4, 3)
    lax.fori_loop(10, 13, dequant, 0)
    load_t.start()
    load_d.start()
    forward(2, 1, 2, 2)
    forward(4, 0, 4, 3)
    for back, way, slot in ((-3, 1, 3), (3, 3, 7), (-4, 2, 4)):
        for h in range(2):
            copy_y(yo, back, way, h).wait_recv()
            go(copy_c(slot, 1, back, core, h))
    for yy in range(2):
        for slot in range(8):
            for h in range(2):
                copy_c(slot, yy, slot if slot < 5 else 4 - slot, co, h).wait_recv()

    def x_far(c, x_first):
        if x_first:
            a, b = pb.at[c, x2, 0], pb.at[c, x2, 1]
            to_a, to_b = r1.at[c, 0], r1.at[c, 1]
        else:
            a, b = pb.at[c, x2, yh, pl.ds(0, 32)], pb.at[c, x2, yh, pl.ds(32, 32)]
            to_a, to_b = r1.at[c, 0, pl.ds(0, 32)], r1.at[c, 1, pl.ds(0, 32)]
        return (
            remote(a, to_a, r1s.at[c, 0], r1r.at[c, 0], dev_r),
            remote(b, to_b, r1s.at[c, 1], r1r.at[c, 1], dev_l),
        )

    def x_near(c, x_first):
        if x_first:
            a, b, to_a, to_b = pb.at[c, xr], pb.at[c, xl], r2.at[c, 0], r2.at[c, 1]
        else:
            a, b, to_a, to_b = pb.at[c, xr, yh], pb.at[c, xl, yh], r2.at[c, 0, 0], r2.at[c, 1, 0]
        return (
            remote(a, to_a, r2s.at[c, 0], r2r.at[c, 0], dev_r),
            remote(b, to_b, r2s.at[c, 1], r2r.at[c, 1], dev_l),
        )

    def y_swap(c, x_first):
        if x_first:
            return remote(s3.at[c], r3.at[c], r3s.at[c], r3r.at[c], dev_h)
        return remote(pb.at[c, :, ho], ry.at[c], r3s.at[c], r3r.at[c], dev_h)

    def add_far(c, x_first):
        arrive, leave = x_far(c, x_first), x_near(c, x_first)
        for side, at in ((0, xr), (1, xl)):
            arrive[side].wait_recv()
            if x_first:
                pb[c, at, side] = (pb[c, at, side].astype(F32) + r1[c, side].astype(F32)).astype(BF16)
            else:
                rows = pl.ds(32 * side, 32)
                pb[c, at, yh, rows] = (
                    pb[c, at, yh, rows].astype(F32) + r1[c, side, 0:32].astype(F32)
                ).astype(BF16)
            leave[side].start()

    def multiply(x_first, c, carry):
        both = jnp.dot(xg[...].reshape(512, 2048), w[c], preferred_element_type=F32)
        pb[c] = both.astype(BF16).reshape(4, 2, 64, 256)
        for copy in x_far(c, True) if x_first else (y_swap(c, False),):
            copy.start()
        return carry

    def stage_two(x_first, c, carry):
        if x_first:
            add_far(c, True)
        else:
            y_swap(c, False).wait_recv()
            for at in range(4):
                pb[c, at, yh] = (pb[c, at, yh].astype(F32) + ry[c, at].astype(F32)).astype(BF16)
            for copy in x_far(c, False):
                copy.start()
        return carry

    def stage_three(x_first, c, carry):
        if x_first:
            arrive = x_near(c, True)
            arrive[0].wait_recv()
            arrive[1].wait_recv()

            def total(half):
                return pb[c, x, half].astype(F32) + r2[c, 0, half].astype(F32) + r2[c, 1, half].astype(F32)

            s3[c] = total(ho).astype(BF16)
            y_swap(c, True).start()
            own[c] = total(yh)
        else:
            add_far(c, False)
        return carry

    def owner(i):
        u = lax.rem(i, 32)
        return 2 * lax.rem(u, 16) + lax.div(u, 16)

    def a2a_out(i):
        slot = lax.div(i, 32)
        return remote(hid.at[i], gin.at[slot, t], as_.at[i], ar.at[slot, t], (dp, owner(i)))

    def stage_four(x_first, c, carry):
        if x_first:
            y_swap(c, True).wait_recv()
            full = own[c] + r3[c].astype(F32)
        else:
            arrive = x_near(c, False)
            arrive[0].wait_recv()
            arrive[1].wait_recv()
            full = pb[c, x, yh].astype(F32) + r2[c, 0, 0].astype(F32) + r2[c, 1, 0].astype(F32)
        gate, up = full[:, :128], full[:, 128:]
        signs = flip[pl.ds(pl.multiple_of(128 * c, 128), 128)].reshape(1, 128)
        hidden = (gate / (1.0 + jnp.exp(-gate)) * up).astype(BF16).astype(F32)
        flipped = jnp.where(signs == 1, hidden, -hidden).astype(BF16)
        for h in range(4):
            hid[4 * c + h] = flipped[16 * h : 16 * h + 16]

            @pl.when(owner(4 * c + h) != t)
            def _():
                a2a_out(4 * c + h).start()

        return carry

    mine = 16 * core + lax.div(t, 2)

    def tile(i):
        rows = pl.ds(pl.multiple_of(16 * lax.rem(i, 4), 16), 16)
        return rg.at[dp, rows, pl.ds(pl.multiple_of(128 * lax.div(i, 4), 128), 128)]

    def a2a_back(slot, o):
        i = mine + 32 * slot
        return remote(gout.at[slot, o], tile(i), bs.at[slot, o], br.at[i], (dp, o))

    def handle(first, count):
        for slot in range(2):
            i = mine + 32 * slot
            if 32 * slot >= 4 * (first + count) or 32 * slot + 32 <= 4 * first:
                continue

            @pl.when((i >= 4 * first) & (i < 4 * (first + count)))
            def _():
                gin[slot, t] = hid[i]

                def arrive(k, carry):
                    o = lax.rem(t + k, 32)
                    remote(gin.at[slot, o], gin.at[slot, o], as_.at[0], ar.at[slot, o], (dp, o)).wait_recv()
                    return carry

                lax.fori_loop(1, 32, arrive, 0)
                values = [gin[slot, g].astype(F32) for g in range(32)]
                for bit in range(5):
                    step = 1 << bit
                    values = [
                        values[g] + values[g + step] if g & step == 0 else values[g - step] - values[g]
                        for g in range(32)
                    ]
                for g in range(32):
                    gout[slot, g] = values[g].astype(BF16)

                def send(k, carry):
                    a2a_back(slot, lax.rem(t + k, 32)).start()
                    return carry

                lax.fori_loop(1, 32, send, 0)
                tile(i)[...] = gout[slot, t]

    def spread(g, slot, at, half, device, rows=slice(0, 64)):
        first, count = GROUPS[g][:2]
        block = rg.at[2 * at + half, pl.ds(rows.start, rows.stop - rows.start), pl.ds(128 * first, 128 * count)]
        return remote(block, block, ags.at[g, slot], agr.at[g, slot], device)

    top, low = slice(0, 32), slice(32, 64)

    def gather_one(g):
        first, count = GROUPS[g][:2]

        def arrive(i, carry):
            @pl.when(owner(i) != t)
            def _():
                remote(gout.at[0, 0], tile(i), bs.at[0, 0], br.at[i], (dp, owner(i))).wait_recv()

            return carry

        lax.fori_loop(4 * first, 4 * (first + count), arrive, 0)
        for slot, device in enumerate((dev_r, dev_l, dev_h)):
            go(spread(g, slot, x, yh, device))

    def gather_two(g):
        if GROUPS[g][3]:
            spread(g, 0, xl, yh, dev_r).wait_recv()
            go(spread(g, 3, xl, yh, dev_r, top))
            go(spread(g, 5, xl, yh, dev_h))
            spread(g, 1, xr, yh, dev_l).wait_recv()
            go(spread(g, 4, xr, yh, dev_l, low))
            go(spread(g, 6, xr, yh, dev_h))
        else:
            spread(g, 0, xl, yh, dev_r).wait_recv()
            go(spread(g, 5, xl, yh, dev_r))
            spread(g, 2, x, ho, dev_h).wait_recv()
            go(spread(g, 3, x, ho, dev_r))
            go(spread(g, 4, x, ho, dev_l))

    def gather_three(g):
        if GROUPS[g][3]:
            spread(g, 3, x2, yh, dev_r, top).wait_recv()
            spread(g, 4, x2, yh, dev_l, low).wait_recv()
            go(spread(g, 7, x2, yh, dev_h))
        else:
            spread(g, 4, xr, ho, dev_l).wait_recv()
            go(spread(g, 6, xr, ho, dev_l))

    def gather_wait(g):
        if GROUPS[g][3]:
            spread(g, 2, x, ho, dev_h).wait_recv()
            spread(g, 5, xl, ho, dev_h).wait_recv()
            spread(g, 6, xr, ho, dev_h).wait_recv()
            spread(g, 7, x2, ho, dev_h).wait_recv()
        else:
            spread(g, 1, xr, yh, dev_l).wait_recv()
            spread(g, 3, xl, ho, dev_r).wait_recv()
            spread(g, 5, x2, yh, dev_r).wait_recv()
            spread(g, 6, x2, ho, dev_l).wait_recv()

    def inner(g):
        gather_wait(g)
        first, count = GROUPS[g][:2]
        rows = slice(128 * first, 128 * (first + count))

        def columns(cols):
            part = jnp.dot(
                rg[:, :, rows].reshape(512, 128 * count), table[rows, cols], preferred_element_type=F32
            )
            if g != ORDER[0]:
                part = part + acc[:, cols]
            if g != ORDER[-1]:
                acc[:, cols] = part
            else:
                rot[:, cols] = (part * FF**-0.5).astype(BF16)

        def step(n, carry):
            columns(pl.ds(pl.multiple_of(256 * n, 256), 256))
            return carry

        lax.fori_loop(0, 6, step, 0)
        columns(pl.ds(1536, 128))

    def dequant_down(c, carry):
        cols = pl.ds(pl.multiple_of(128 * c, 128), 128)
        scales = ds_[:, cols].astype(F32)
        for g in range(13):
            words = dbuf[32 * g : 32 * g + 32, cols]
            for j in range(4):
                row = 416 * j + 32 * g
                wd[row : row + 32, cols] = unpack(words, scales[g : g + 1], j)
        return carry

    def run(stage, g):
        first, count, x_first = GROUPS[g][:3]
        lax.fori_loop(first, first + count, functools.partial(stage, x_first), 0)

    def H(g):
        handle(GROUPS[g][0], GROUPS[g][1])

    M, S2, S3, S4 = (functools.partial(run, stage) for stage in (multiply, stage_two, stage_three, stage_four))
    T1, T2, T3, I = gather_one, gather_two, gather_three, inner

    def unpack_down():
        load_t.wait()
        load_d.wait()
        lax.fori_loop(0, 16, dequant_down, 0)

    M(0), M(3), M(1), S2(0), M(2), S2(1)
    unpack_down()
    S3(0), S2(3), S2(2), S4(0), S3(1), S3(3), H(0), S4(1), S3(2), T1(0), H(1), S4(3), T2(0), H(3), T1(1), S4(2), T3(0)
    H(2), T1(3), T2(1), I(0), T2(3), T3(1), T1(2), T3(3), T2(2), I(1), T3(2), I(3), I(2)

    def pair(c):
        return remote(qb.at[c, co], rc.at[c], ccs.at[c], ccr.at[c], dev_c)

    def one(c):
        return (
            remote(qb.at[c, core, 0, zat(4)], rz1.at[0, c], zs.at[0, 0, c], zr.at[0, 0, c], dev_u),
            remote(qb.at[c, core, 1, zat(4)], rz1.at[1, c], zs.at[1, 0, c], zr.at[1, 0, c], dev_d),
        )

    def ring(r, c):
        k = 5 - r
        return (
            remote(qb.at[c, core, :, zat(k)], rz.at[0, r - 2, c], zs.at[0, r - 1, c], zr.at[0, r - 1, c], dev_u),
            remote(qb.at[c, core, :, zat(-k)], rz.at[1, r - 2, c], zs.at[1, r - 1, c], zr.at[1, r - 1, c], dev_d),
        )

    def across(c):
        return remote(tot.at[c, yo], rl.at[c], yys.at[c], yyr.at[c], dev_y)

    def down(c, carry):
        for part in range(2):
            cols = pl.ds(pl.multiple_of(WC * c + 256 * part, 256), 256)
            terms = jnp.dot(rot[...], wd[:, cols], preferred_element_type=F32).astype(BF16)
            for cc in range(2):
                for yy in range(2):
                    for zz in range(8):
                        row = 16 * (16 * yy + 2 * zz + cc)
                        qb[c, cc, yy, zz, :, 256 * part : 256 * part + 256] = terms[row : row + 16]
        pair(c).start()
        return carry

    def round_one(c, carry):
        pair(c).wait_recv()
        qb[c, core] = (qb[c, core].astype(F32) + rc[c].astype(F32)).astype(BF16)
        for copy in one(c):
            copy.start()
        return carry

    def round_two(c, carry):
        for side in range(2):
            one(c)[side].wait_recv()
            at = zat(3 - 6 * side)
            qb[c, core, side, at] = (qb[c, core, side, at].astype(F32) + rz1[side, c].astype(F32)).astype(BF16)
            ring(2, c)[side].start()
        return carry

    def round_more(r, c, carry):
        for side in range(2):
            ring(r - 1, c)[side].wait_recv()
            at = zat((5 - r) * (1 - 2 * side))
            for yy in range(2):
                qb[c, core, yy, at] = (
                    qb[c, core, yy, at].astype(F32) + rz[side, r - 3, c, yy].astype(F32)
                ).astype(BF16)
            ring(r, c)[side].start()
        return carry

    def round_last(c, carry):
        for side in range(2):
            ring(4, c)[side].wait_recv()
        for yy in range(2):
            tot[c, yy] = (
                qb[c, core, yy, z].astype(F32) + rz[0, 2, c, yy].astype(F32) + rz[1, 2, c, yy].astype(F32)
            ).astype(BF16)
        across(c).start()
        return carry

    def finish(c, carry):
        across(c).wait_recv()
        cols = pl.ds(pl.multiple_of(WC * c, WC), WC)
        out[:, cols] = (tot[c, yl].astype(F32) + rl[c].astype(F32)).astype(BF16)
        return carry

    def start(c, carry):
        down(c, carry)

        @pl.when(c >= 1)
        def _():
            round_one(c - 1, carry)

        @pl.when(c >= 2)
        def _():
            round_two(c - 2, carry)

        return carry

    lax.fori_loop(0, NC, start, 0)
    round_one(NC - 1, 0)
    round_two(NC - 2, 0)
    round_two(NC - 1, 0)
    steps = (functools.partial(round_more, 3), functools.partial(round_more, 4), round_last, finish)
    for step in steps:
        lax.fori_loop(0, NC, step, 0)

    def drain_down(c, carry):
        for copy in (pair(c),) + one(c) + ring(2, c) + ring(3, c) + ring(4, c) + (across(c),):
            copy.wait_send()
        return carry

    def drain_up(x_first, c, carry):
        for copy in x_far(c, x_first) + x_near(c, x_first) + (y_swap(c, x_first),):
            copy.wait_send()
        for h in range(4):

            @pl.when(owner(4 * c + h) != t)
            def _():
                a2a_out(4 * c + h).wait_send()

        return carry

    lax.fori_loop(0, NC, drain_down, 0)
    for g in range(len(GROUPS)):
        run(drain_up, g)

    for slot in range(2):

        @pl.when(mine + 32 * slot < 4 * CH)
        def _():
            def drain_back(k, carry):
                a2a_back(slot, lax.rem(t + k, 32)).wait_send()
                return carry

            lax.fori_loop(1, 32, drain_back, 0)

    for copy in sends:
        copy.wait_send()


def per_device(
    tokens, gate_codes, gate_scales, up_codes, up_scales, down_codes, down_scales, flip_signs
):
    vm = pl.BlockSpec(memory_space=pltpu.VMEM)
    hbm = pl.BlockSpec(memory_space=pl.ANY)
    dma = pltpu.SemaphoreType.DMA
    ng = len(GROUPS)
    return pl.pallas_call(
        kernel,
        out_shape=jax.ShapeDtypeStruct((16, 2048), BF16),
        in_specs=[vm, hbm, hbm, hbm, vm, vm, vm, vm, hbm],
        out_specs=vm,
        scratch_shapes=[
            pltpu.VMEM((512, 2048), jnp.int32),
            pltpu.VMEM((512, 1664), jnp.int32),
            pltpu.VMEM((CH, 2048, 256), BF16),
            pltpu.VMEM((2, 8, 2, 16, 2048), BF16),
            pltpu.VMEM((CH, 4, 2, 64, 256), BF16),
            pltpu.VMEM((CH, 2, 64, 256), BF16),
            pltpu.VMEM((CH, 2, 2, 64, 256), BF16),
            pltpu.VMEM((CH, 4, 64, 256), BF16),
            pltpu.VMEM((CH, 64, 256), BF16),
            pltpu.VMEM((CH, 64, 256), BF16),
            pltpu.VMEM((CH, 64, 256), F32),
            pltpu.VMEM((1664, 1664), BF16),
            pltpu.VMEM((4 * CH, 16, 128), BF16),
            pltpu.VMEM((2, 32, 16, 128), BF16),
            pltpu.VMEM((2, 32, 16, 128), BF16),
            pltpu.VMEM((8, 64, 1664), BF16),
            pltpu.VMEM((512, 1664), F32),
            pltpu.VMEM((1664, 2048), BF16),
            pltpu.VMEM((512, 1664), BF16),
            pltpu.VMEM((NC, 2, 2, 8, 16, WC), BF16),
            pltpu.VMEM((NC, 2, 8, 16, WC), BF16),
            pltpu.VMEM((2, NC, 16, WC), BF16),
            pltpu.VMEM((2, 3, NC, 2, 16, WC), BF16),
            pltpu.VMEM((NC, 2, 16, WC), BF16),
            pltpu.VMEM((NC, 16, WC), BF16),
            dma((4,)), dma((4, 2)), dma((4, 2)),
            dma((4, 2, 2)), dma((4, 2, 2)), dma((3, 2, 2)), dma((3, 2, 2)), dma((8, 2, 2)), dma((8, 2, 2)),
            dma((4 * CH,)), dma((2, 32)), dma((2, 32)), dma((4 * CH,)),
            dma((CH, 2)), dma((CH, 2)), dma((CH, 2)), dma((CH, 2)), dma((CH,)), dma((CH,)),
            dma((ng, 8)), dma((ng, 8)),
            dma((NC,)), dma((NC,)), dma((2, 4, NC)), dma((2, 4, NC)), dma((NC,)), dma((NC,)),
        ],
        compiler_params=pltpu.CompilerParams(
            collective_id=0, has_side_effects=True, vmem_limit_bytes=VMEM_LIMIT
        ),
        cost_estimate=pl.CostEstimate(flops=14 * 10**9, bytes_accessed=2 * 10**7, transcendentals=10**5),
    )(
        tokens, gate_codes, up_codes, down_codes, gate_scales, up_scales, down_scales,
        flip_signs, jnp.asarray(inner_table(), dtype=BF16),
    )


def solution(mesh):
    return jax.shard_map(
        per_device,
        mesh=mesh,
        in_specs=(
            P("tensor", "dp"),
            P("dp", "tensor"),
            P("dp", "tensor"),
            P("dp", "tensor"),
            P("dp", "tensor"),
            P("tensor", "dp"),
            P("tensor", "dp"),
            P("tensor"),
        ),
        out_specs=P("tensor", "dp"),
        check_vma=False,
    )
```

time: 418 us -> 124 us (0.30)
  waiting for transfers between devices: 259 us -> 0 us
  Pallas kernels: 0 us -> 121 us
  local copies, waits for them, and re-layouts: 81.1 us -> 1.47 us
  other arithmetic: 26.8 us -> 0 us
  matrix products: 25.4 us -> 0 us
  between operations: 13.3 us -> 0.01 us
  starting transfers between devices: 11.1 us -> 0 us
    pallas_call x0 -> x1, Pallas kernels: none -> 121 us  [per_device(): pl.pallas_call(kernel, out_shape=jax.ShapeDtypeStruct((16, 2048), BF16),...]
    reduce_scatter x1 -> x0, waiting for transfers between devices: 118 us -> none  [per_device(): lax.psum_scatter(terms.astype(jnp.bfloat16), 'tensor', scatter_dimension=...]
    unnamed x5 -> x0, waiting for transfers between devices: 86.8 us -> none
    shift_right_arithmetic x10 -> x0, local copies, waits for them, and re-layouts: 75.9 us -> none  [dequant(): jnp.right_shift(code_words[:, None, :], shifts[None, :, None])]
    ppermute x5 -> x0, waiting for transfers between devices: 30.5 us -> none  [from_partner(): lax.ppermute(value, axis, [(i, i ^ 1 << bit) for i in range(lax.axis_size...]
    convert_element_type x11 -> x0, other arithmetic: 26.8 us -> none  [the longest x2 25.4 us: dequant(): return (levels.astype(jnp.float32) * spread).astype(jnp.bfloat16)]
    dot_general x3 -> x0, matrix products: 25.4 us -> none  [the longest x1 12.8 us: per_device(): jnp.dot(all_rows, both_weights, preferred_element_type=jnp.float32)]
    all_gather x2 -> x0, waiting for transfers between devices: 23.6 us -> none  [the longest x1 19.2 us: per_device(): lax.all_gather(rotated, 'dp', axis=0, tiled=True)]
  transfers between devices with their start and end apart: 9 -> 0, of which waited for: 9 -> 0; matrix products, arithmetic and copies ran while one was open for 24% -> 0% of each run, Pallas kernels for 0% -> 0%
where the time goes in v2:
time: 124 us; the launch traced here: 122 us
  Pallas kernels  121 us (98%)
  local copies, waits for them, and re-layouts  1.47 us (1%)
    pallas_call x1, Pallas kernels, per_device(): pl.pallas_call(kernel, out_shape=jax.ShapeDtypeStruct((16, 2048), BF16),...  121 us

profile of v2, /device:TPU:2, one launch (start us, length us, event | category | flops | bytes accessed | tf_op | source)
XLA Modules:
  0.0 122.2 jit_solution(9993954829219214122)
XLA Ops:
  0.0 120.7 %shard_map.91 = bf16[16,2048]{1,0:T(8,128)(2,1)} custom-call(bf16[16,2048]{1,0:T(8,128)(2,1)} %tok.1, s32[512,1664]{1,0:T(8,128)} %gcodes.1, s32[512,1664]{1,0:T(8,128)} %ucodes.1, s32[416,2048]{1,0:T(8,128)} %dcodes.1, bf16[16,1664]{1,0:T(8,128)(2,1)} %gs.1, bf16[16,1664]{1,0:T(8,128)(2,1)} %us.1, bf16[13,2048]{1,0:T(8,128)(2,1)} %ds_.1, s32[1664]{0:T(1024)} %flip.1, ...), custom_call_target="tpu_custom_call" | custom-call | flops 14000000000 | bytes 20000000 | tf_op jit(solution)/shard_map/pallas_call | solution.py:613
  120.7 1.5 %copy.11 = bf16[16,2048]{1,0:T(8,128)(2,1)} copy(bf16[16,2048]{1,0:T(8,128)(2,1)} %shard_map.91) | data formatting | bytes 131072

commit v3 on v2

v3 whole, which is shorter than its diff:
```python
import functools

import jax
import jax.numpy as jnp
import numpy as np
from jax import lax
from jax.experimental import pallas as pl
from jax.experimental.pallas import tpu as pltpu
from jax.sharding import PartitionSpec as P

FF = 53248
KB = 52
BLK = 32
MESH = pl.DeviceIdType.MESH
BF16 = jnp.bfloat16
F32 = jnp.float32
VMEM_LIMIT = 60 * 1024 * 1024


def paley_table():
    field_square = np.zeros(25, dtype=np.int64)
    for first_part in range(5):
        for second_part in range(5):
            if first_part == 0 and second_part == 0:
                continue
            real_part = (first_part * first_part + 2 * second_part * second_part) % 5
            root_part = 2 * first_part * second_part % 5
            field_square[real_part + 5 * root_part] = 1
    character = np.where(field_square == 1, 1, -1)
    character[0] = 0
    jacobsthal = np.zeros((25, 25), dtype=np.int64)
    for left_item in range(25):
        for right_item in range(25):
            diff_real = (left_item % 5 - right_item % 5) % 5
            diff_root = (left_item // 5 - right_item // 5) % 5
            jacobsthal[left_item, right_item] = character[diff_real + 5 * diff_root]
    conference = np.zeros((26, 26), dtype=np.int64)
    conference[0, 1:] = 1
    conference[1:, 0] = 1
    conference[1:, 1:] = jacobsthal
    outer_part = np.array([[1, -1], [-1, -1]], dtype=np.int64)
    inner_part = np.array([[1, 1], [1, -1]], dtype=np.int64)
    return np.kron(conference, outer_part) + np.kron(np.eye(26, dtype=np.int64), inner_part)


def sylvester_static(order_size):
    position = np.arange(order_size)
    parity = np.zeros((order_size, order_size), dtype=np.int64)
    for bit_place in range(max(order_size.bit_length() - 1, 0)):
        parity = parity + (position[:, None] >> bit_place & position[None, :] >> bit_place & 1)
    return 1 - 2 * (parity & 1)


def inner_table():
    table = np.kron(paley_table(), sylvester_static(BLK))
    order = (4 * np.arange(416)[None, :] + np.arange(4)[:, None]).reshape(-1)
    return table[:, order].astype(np.float32)


def remote(src, dst, send_sem, recv_sem, device):
    return pltpu.make_async_remote_copy(
        src_ref=src, dst_ref=dst, send_sem=send_sem, recv_sem=recv_sem, device_id=device, device_id_type=MESH
    )


def place():
    dp = lax.axis_index("dp")
    t = lax.axis_index("tensor")
    x, yh = lax.div(dp, 2), lax.rem(dp, 2)
    yl, z, core = lax.div(t, 16), lax.rem(lax.div(t, 2), 8), lax.rem(t, 2)
    return dp, t, x, yh, yl, z, core


def unpack(words, scale, j):
    levels = (words & (7 << (3 * j))).astype(F32).astype(BF16) - jnp.asarray(4.0 * 8.0**j, BF16)
    return levels * (scale * 8.0**-j).astype(BF16)


CH = 13
GROUPS = ((0, 3, False, "2"), (3, 3, True, "y"), (6, 3, False, "y"), (9, 4, True, "x"))
ORDER = (1, 0, 2, 3)
NC = 4
WC = 512


def kernel(
    tok, gcodes, ucodes, dcodes, gs, us, ds_, flip, table_hbm, out,
    cbuf, ubuf, w, xg, pb, r1, r2, ry, s3, r3, own,
    table, hid, gin, gout, rg, acc, wd,
    qb, rc, rz1, rz, rl,
    ld, sd, as_, bs, ar, br, cr, yr, pr, sr, r1r, r2r, r3r, agr, ccr, zr, yyr,
):
    dp, t, x, yh, yl, z, core = place()
    ho, yo, co = 1 - yh, 1 - yl, 1 - core
    sign = 1 - 2 * core
    tid = lambda a, b, c: a * 16 + b * 2 + c
    zat = lambda k: lax.rem(z + k + 8, 8)
    zsg = lambda k: lax.rem(z + sign * k + 8, 8)
    xr, xl, x2 = lax.rem(x + 1, 4), lax.rem(x + 3, 4), lax.rem(x + 2, 4)
    dev_y, dev_c = (dp, tid(yo, z, core)), (dp, tid(yl, z, co))
    dev_p, dev_s = (dp, tid(yl, zsg(1), core)), (dp, tid(yl, zsg(-1), core))
    dev_u, dev_d = (dp, tid(yl, zat(1), core)), (dp, tid(yl, zat(-1), core))
    dev_r, dev_l, dev_h = (xr * 2 + yh, t), (xl * 2 + yh, t), (x * 2 + ho, t)

    barrier = pltpu.get_barrier_semaphore()
    for device in (dev_r, dev_l, dev_h):
        pl.semaphore_signal(barrier, inc=1, device_id=device, device_id_type=MESH)

    def greet(k, carry):
        pl.semaphore_signal(barrier, inc=1, device_id=(dp, lax.rem(t + k, 32)), device_id_type=MESH)
        return carry

    lax.fori_loop(1, 32, greet, 0)
    gbuf, dbuf = cbuf.at[:, pl.ds(0, 1664)], cbuf.at[pl.ds(0, 416)]
    load_g = pltpu.make_async_copy(gcodes, gbuf, ld.at[0])
    load_u = pltpu.make_async_copy(ucodes, ubuf, ld.at[1])
    load_t = pltpu.make_async_copy(table_hbm, table, ld.at[2])
    load_d = pltpu.make_async_copy(dcodes, dbuf, ld.at[3])
    load_g.start()
    load_u.start()

    rows_i = lax.broadcasted_iota(jnp.int32, (512, 512), 0)
    cols_i = lax.broadcasted_iota(jnp.int32, (512, 512), 1)
    pick = jnp.where(rows_i == 4 * (cols_i % 128) + cols_i // 128, 1.0, 0.0).astype(BF16)
    for q in range(4):
        cols = slice(512 * q, 512 * q + 512)
        xg[yl, z, core, :, cols] = jnp.dot(tok[:, cols], pick, preferred_element_type=F32).astype(BF16)

    pl.semaphore_wait(barrier, 34)

    sent = [0, 0, 0, 0]

    def size(ref):
        return int(np.prod(ref.shape)) * 2

    def push(phase, src, dst, recv_sem, device, times=1):
        sent[phase] += size(src) * times
        return remote(src, dst, sd.at[phase], recv_sem, device)

    def settle(phase):
        rows = sent[phase] // 512
        for outer in range(1, CH + 1):
            if rows % outer == 0 and rows // outer % 16 == 0 and rows // outer <= 2048:
                span = w.at[pl.ds(0, outer), pl.ds(0, rows // outer)]
                pltpu.make_async_copy(span, span, sd.at[phase]).wait()
                return
        raise ValueError(rows)

    def landed(ref, sem):
        pltpu.make_async_copy(ref, ref, sem).wait()

    yv = (yl, yo)

    def piece(y, back, c, h):
        return xg.at[y, zsg(back), c, :, pl.ds(1024 * h, 1024)]

    def copy_y(y, back, slot, h):
        block = piece(y, back, core, h)
        return block, yr.at[slot, h], dev_y

    def copy_p(k, yy, away, h):
        block = piece(yv[yy], -away, core, h)
        return block, pr.at[k - 1, yy, h], dev_p

    def copy_s(k, yy, away, h):
        block = piece(yv[yy], away, core, h)
        return block, sr.at[k - 1, yy, h], dev_s

    def copy_c(slot, yy, back, h):
        return piece(yv[yy], back, core, h), cr.at[0], dev_c

    def go(copy):
        block, sem, device = copy
        push(0, block, block, sem, device).start()

    def come(copy):
        landed(copy[0], copy[1])

    def dequant(c, carry):
        cols = pl.ds(pl.multiple_of(128 * c, 128), 128)
        for side, (buf, sc) in enumerate(((gbuf, gs), (ubuf, us))):
            scales = sc[:, cols].astype(F32)
            for g in range(16):
                words = buf[32 * g : 32 * g + 32, cols]
                for j in range(4):
                    row = 512 * (g // 4) + 128 * j + 32 * (g % 4)
                    w[c, row : row + 32, 128 * side : 128 * side + 128] = unpack(words, scales[g : g + 1], j)
        return carry

    def ring(k, yy, h, reach_p=4, reach_s=3):
        if k <= reach_p:
            come(copy_p(k, yy, k, h))
            if k < 4:
                go(copy_p(k + 1, yy, k, h))
            if h == 0:
                go(copy_y(yl, -k, k, h))
            go(copy_c(k, yy, -k, h))
        if k <= reach_s:
            come(copy_s(k, yy, k, h))
            if k < 3:
                go(copy_s(k + 1, yy, k, h))
            if h == 0:
                go(copy_y(yl, k, 4 + k, h))
            go(copy_c(4 + k, yy, k, h))

    go(copy_y(yl, 0, 0, 1))
    for h in range(2):
        go(copy_p(1, 0, 0, h))
        go(copy_s(1, 0, 0, h))
    go(copy_y(yl, 0, 0, 0))
    for h in range(2):
        go(copy_c(0, 0, 0, h))
    load_g.wait()
    load_u.wait()
    lax.fori_loop(0, 2, dequant, 0)
    ring(1, 0, 0)
    come(copy_y(yo, 0, 0, 1))
    go(copy_p(1, 1, 0, 1))
    go(copy_s(1, 1, 0, 1))
    ring(1, 0, 1)
    come(copy_y(yo, 0, 0, 0))
    for h in range(2):
        go(copy_c(0, 1, 0, h))
    lax.fori_loop(2, 4, dequant, 0)
    ring(2, 0, 0)
    ring(1, 1, 1)
    ring(2, 0, 1)
    lax.fori_loop(4, 6, dequant, 0)
    ring(3, 0, 0)
    ring(2, 1, 1)
    ring(3, 0, 1)
    lax.fori_loop(6, 9, dequant, 0)
    ring(4, 0, 0)
    ring(3, 1, 1)
    ring(4, 0, 1)
    lax.fori_loop(9, 13, dequant, 0)
    load_t.start()
    load_d.start()
    for back, way, slot in ((-1, 1, 1), (1, 5, 5), (-2, 2, 2), (2, 6, 6), (-3, 3, 3), (3, 7, 7), (-4, 4, 4)):
        come(copy_y(yo, back, way, 0))
        go(copy_c(slot, 1, back, 0))
    ring(4, 1, 1)
    landed(w.at[0], cr.at[0])

    def x_far(c, x_first, times):
        if x_first:
            a, b = pb.at[c, x2, 0], pb.at[c, x2, 1]
            to_a, to_b = r1.at[c, 0], r1.at[c, 1]
        else:
            a, b = pb.at[c, x2, yh, pl.ds(0, 32)], pb.at[c, x2, yh, pl.ds(32, 32)]
            to_a, to_b = r1.at[c, 0, pl.ds(0, 32)], r1.at[c, 1, pl.ds(0, 32)]
        push(1, a, to_a, r1r.at[c], dev_r, times).start()
        push(1, b, to_b, r1r.at[c], dev_l, times).start()

    def x_near(c, x_first, times):
        if x_first:
            a, b, to_a, to_b = pb.at[c, xr], pb.at[c, xl], r2.at[c, 0], r2.at[c, 1]
        else:
            a, b, to_a, to_b = pb.at[c, xr, yh], pb.at[c, xl, yh], r2.at[c, 0, 0], r2.at[c, 1, 0]
        push(1, a, to_a, r2r.at[c], dev_r, times).start()
        push(1, b, to_b, r2r.at[c], dev_l, times).start()

    def add_far(c, x_first, times):
        landed(r1.at[c] if x_first else r1.at[c, 0], r1r.at[c])
        for side, at in ((0, xr), (1, xl)):
            if x_first:
                pb[c, at, side] = (pb[c, at, side].astype(F32) + r1[c, side].astype(F32)).astype(BF16)
            else:
                rows = pl.ds(32 * side, 32)
                pb[c, at, yh, rows] = (
                    pb[c, at, yh, rows].astype(F32) + r1[c, side, 0:32].astype(F32)
                ).astype(BF16)
        x_near(c, x_first, times)

    def multiply(x_first, times, c, carry):
        both = jnp.dot(xg[...].reshape(512, 2048), w[c], preferred_element_type=F32)
        pb[c] = both.astype(BF16).reshape(4, 2, 64, 256)
        if x_first:
            x_far(c, True, times)
        else:
            push(1, pb.at[c, :, ho], ry.at[c], r3r.at[c], dev_h, times).start()
        return carry

    def stage_two(x_first, times, c, carry):
        if x_first:
            add_far(c, True, times)
        else:
            landed(ry.at[c], r3r.at[c])
            for at in range(4):
                pb[c, at, yh] = (pb[c, at, yh].astype(F32) + ry[c, at].astype(F32)).astype(BF16)
            x_far(c, False, times)
        return carry

    def stage_three(x_first, times, c, carry):
        if x_first:
            landed(r2.at[c], r2r.at[c])

            def total(half):
                return pb[c, x, half].astype(F32) + r2[c, 0, half].astype(F32) + r2[c, 1, half].astype(F32)

            s3[c] = total(ho).astype(BF16)
            push(1, s3.at[c], r3.at[c], r3r.at[c], dev_h, times).start()
            own[c] = total(yh)
        else:
            add_far(c, False, times)
        return carry

    def owner(i):
        u = lax.rem(i, 32)
        return 2 * lax.rem(u, 16) + lax.div(u, 16)

    def a2a_out(i):
        slot = lax.div(i, 32)
        return remote(hid.at[i], gin.at[slot, t], as_.at[0], ar.at[slot], (dp, owner(i)))

    def stage_four(x_first, times, c, carry):
        if x_first:
            landed(r3.at[c], r3r.at[c])
            full = own[c] + r3[c].astype(F32)
        else:
            landed(r2.at[c, 0], r2r.at[c])
            full = pb[c, x, yh].astype(F32) + r2[c, 0, 0].astype(F32) + r2[c, 1, 0].astype(F32)
        gate, up = full[:, :128], full[:, 128:]
        signs = flip[pl.ds(pl.multiple_of(128 * c, 128), 128)].reshape(1, 128)
        hidden = (gate / (1.0 + jnp.exp(-gate)) * up).astype(BF16).astype(F32)
        flipped = jnp.where(signs == 1, hidden, -hidden).astype(BF16)
        for h in range(4):
            hid[4 * c + h] = flipped[16 * h : 16 * h + 16]

            @pl.when(owner(4 * c + h) != t)
            def _():
                a2a_out(4 * c + h).start()

        return carry

    mine = 16 * core + lax.div(t, 2)

    def tile(i):
        rows = pl.ds(pl.multiple_of(16 * lax.rem(i, 4), 16), 16)
        return rg.at[dp, rows, pl.ds(pl.multiple_of(128 * lax.div(i, 4), 128), 128)]

    def group_of(i):
        found = 0
        for first, _, _, _ in GROUPS[1:]:
            found = found + jnp.where(i >= 4 * first, 1, 0)
        return found

    def a2a_back(slot, o):
        i = mine + 32 * slot
        return remote(gout.at[slot, o], tile(i), bs.at[slot], br.at[group_of(i)], (dp, o))

    def handle(first, count):
        for slot in range(2):
            i = mine + 32 * slot
            if 32 * slot >= 4 * (first + count) or 32 * slot + 32 <= 4 * first:
                continue

            @pl.when((i >= 4 * first) & (i < 4 * (first + count)))
            def _():
                gin[slot, t] = hid[i]

                landed(gin.at[slot, pl.ds(0, 31)], ar.at[slot])
                values = [gin[slot, g].astype(F32) for g in range(32)]
                for bit in range(5):
                    step = 1 << bit
                    values = [
                        values[g] + values[g + step] if g & step == 0 else values[g - step] - values[g]
                        for g in range(32)
                    ]
                for g in range(32):
                    gout[slot, g] = values[g].astype(BF16)

                def send(k, carry):
                    a2a_back(slot, lax.rem(t + k, 32)).start()
                    return carry

                lax.fori_loop(1, 32, send, 0)
                tile(i)[...] = gout[slot, t]

    def block(g, at, half, rows=slice(0, 64)):
        first, count = GROUPS[g][:2]
        return rg.at[2 * at + half, pl.ds(rows.start, rows.stop - rows.start), pl.ds(128 * first, 128 * count)]

    def blocks(g, n):
        first, count = GROUPS[g][:2]
        return rg.at[pl.ds(0, n), :, pl.ds(128 * first, 128 * count)]

    def spread(g, sem, at, half, device, rows=slice(0, 64)):
        part = block(g, at, half, rows)
        push(2, part, part, agr.at[g, sem], device).start()

    top, low = slice(0, 32), slice(32, 64)

    def gather_one(g):
        first, count, _, kind = GROUPS[g]
        inside = False
        for slot in range(2):
            i = mine + 32 * slot
            inside = inside | ((i >= 4 * first) & (i < 4 * (first + count)))

        @pl.when(inside)
        def _():
            landed(hid.at[pl.ds(0, 4 * count - 1)], br.at[g])

        @pl.when(jnp.logical_not(inside))
        def _():
            landed(hid.at[pl.ds(0, 4 * count)], br.at[g])

        if kind == "x":
            spread(g, 0, x, yh, dev_r)
            spread(g, 1, x, yh, dev_l)
            spread(g, 3, x, yh, dev_h)
        elif kind == "2":
            for sem, device in enumerate((dev_r, dev_l, (x2 * 2 + yh, t), dev_h)):
                spread(g, sem, x, yh, device)
        elif kind == "y":
            spread(g, 0, x, yh, dev_h)
            spread(g, 1, x, yh, dev_r)
            spread(g, 3, x, yh, dev_l)
        else:
            for half in (ho, yh):
                for to in (x2, xr, xl, x):
                    if half is ho or to is not x:
                        spread(g, 3, x, yh, (to * 2 + half, t))

    def gather_two(g):
        if GROUPS[g][3] == "x":
            landed(block(g, xl, yh), agr.at[g, 0])
            spread(g, 2, xl, yh, dev_r, top)
            spread(g, 3, xl, yh, dev_h)
            landed(block(g, xr, yh), agr.at[g, 1])
            spread(g, 2, xr, yh, dev_l, low)
            spread(g, 3, xr, yh, dev_h)
        elif GROUPS[g][3] == "2":
            for sem, at in enumerate((xl, xr, x2)):
                landed(block(g, at, yh), agr.at[g, sem])
                spread(g, 3, at, yh, dev_h)
        else:
            landed(block(g, xl, yh), agr.at[g, 1])
            spread(g, 3, xl, yh, dev_r)
            landed(block(g, x, ho), agr.at[g, 0])
            spread(g, 3, x, ho, dev_r)
            spread(g, 2, x, ho, dev_l)

    def gather_three(g):
        if GROUPS[g][3] == "x":
            landed(block(g, x2, yh), agr.at[g, 2])
            spread(g, 3, x2, yh, dev_h)
        else:
            landed(block(g, xr, ho), agr.at[g, 2])
            spread(g, 3, xr, ho, dev_l)

    def gather_wait(g):
        landed(blocks(g, 7 if GROUPS[g][3] == "d" else 4), agr.at[g, 3])

    def fold(n):
        cols = pl.ds(256 * n, 256)
        for part in range(2):
            rows = pl.ds(832 * part, 832)
            product = jnp.dot(table[rows, :], wd[:, cols], preferred_element_type=F32)
            w[n, rows] = (product * FF**-0.5).astype(BF16)

    def terms_of(g, n):
        first, count = GROUPS[g][:2]
        rows = pl.ds(128 * first, 128 * count)
        units = rg[:, :, 128 * first : 128 * (first + count)].reshape(512, 128 * count)
        return jnp.dot(units, w[n, rows], preferred_element_type=F32)

    def accumulate(g):
        gather_wait(g)

        def step(n, carry):
            cols = pl.ds(pl.multiple_of(256 * n, 256), 256)
            terms = terms_of(g, n)
            acc[:, cols] = terms if g == ORDER[0] else acc[:, cols] + terms
            return carry

        lax.fori_loop(0, 8, step, 0)

    def dequant_down(c, carry):
        cols = pl.ds(pl.multiple_of(128 * c, 128), 128)
        scales = ds_[:, cols].astype(F32)
        for g in range(13):
            words = dbuf[32 * g : 32 * g + 32, cols]
            for j in range(4):
                row = 416 * j + 32 * g
                wd[row : row + 32, cols] = unpack(words, scales[g : g + 1], j)
        return carry

    def run(stage, g):
        first, count, x_first = GROUPS[g][:3]
        lax.fori_loop(first, first + count, functools.partial(stage, x_first, count), 0)

    def H(g):
        handle(GROUPS[g][0], GROUPS[g][1])

    M, S2, S3, S4 = (functools.partial(run, stage) for stage in (multiply, stage_two, stage_three, stage_four))
    T1, T2, T3, W, A = gather_one, gather_two, gather_three, fold, accumulate

    def unpack_down():
        load_t.wait()
        load_d.wait()
        lax.fori_loop(0, 16, dequant_down, 0)

    M(0), M(1), M(3), S2(1), M(2), S2(0), S2(3)
    unpack_down()
    W(0), S3(1), S3(0), W(1), W(2), S2(2), S3(3), W(3), S4(1), S4(0), S3(2), S4(3), S4(2), H(1), H(0), H(3), H(2)
    T1(1), T1(0), W(4), T2(1), T1(2), T1(3), W(5), T2(0), W(6), T3(1), T2(2), W(7), T2(3), A(1), T3(2), T3(3), A(0), A(2)

    def pair(c):
        push(3, qb.at[c, co], rc.at[c], ccr.at[c], dev_c, NC).start()

    def z_one(c, times):
        push(3, qb.at[c, core, 0, zat(4)], rz1.at[c, 0], zr.at[0, c], dev_u, times).start()
        push(3, qb.at[c, core, 1, zat(4)], rz1.at[c, 1], zr.at[0, c], dev_d, times).start()
        push(3, qb.at[c, core, yo, z], rl.at[c], yyr.at[c], dev_y, times).start()

    def down(c):
        for part in range(2):
            n = 2 * c + part
            cols = pl.ds(pl.multiple_of(256 * n, 256), 256)
            terms = (acc[:, cols] + terms_of(ORDER[-1], n)).astype(BF16)
            for cc in range(2):
                for yy in range(2):
                    for zz in range(8):
                        row = 16 * (16 * yy + 2 * zz + cc)
                        qb[c, cc, yy, zz, :, 256 * part : 256 * part + 256] = terms[row : row + 16]
        pair(c)

    def after_pair(times, c):
        landed(rc.at[c], ccr.at[c])
        qb[c, core] = (qb[c, core].astype(F32) + rc[c].astype(F32)).astype(BF16)
        z_one(c, times)

    def z_round(r, c, carry):
        landed(rz1.at[c] if r == 2 else rz.at[r - 3, c], zr.at[r - 2, c])
        for side in range(2):
            at = zat((5 - r) * (1 - 2 * side))
            if r == 2:
                qb[c, core, side, at] = (qb[c, core, side, at].astype(F32) + rz1[c, side].astype(F32)).astype(BF16)
            else:
                for yy in range(2):
                    qb[c, core, yy, at] = (
                        qb[c, core, yy, at].astype(F32) + rz[r - 3, c, side, yy].astype(F32)
                    ).astype(BF16)
            if r < 4:
                push(3, qb.at[c, core, :, at], rz.at[r - 2, c, side], zr.at[r - 1, c], (dev_u, dev_d)[side], NC).start()
            else:
                for row, to in ((0, yl), (1, yo)):
                    device = (dp, tid(to, at, core))
                    push(3, qb.at[c, core, to, at], rz.at[2, c, side, row], zr.at[3, c], device, NC).start()
        return carry

    def finish(c, carry):
        landed(rl.at[c], yyr.at[c])
        landed(rz.at[2, c], zr.at[3, c])
        total = qb[c, core, yl, z].astype(F32) + rl[c].astype(F32)
        for side in range(2):
            for row in range(2):
                total = total + rz[2, c, side, row].astype(F32)
        cols = pl.ds(pl.multiple_of(WC * c, WC), WC)
        out[:, cols] = total.astype(BF16)
        return carry

    gather_wait(ORDER[-1])

    def start(c, carry):
        down(c)

        @pl.when(c > 0)
        def _():
            after_pair(NC - 1, c - 1)

        return carry

    lax.fori_loop(0, NC, start, 0)
    after_pair(1, NC - 1)
    for step in (functools.partial(z_round, 2), functools.partial(z_round, 3), functools.partial(z_round, 4), finish):
        lax.fori_loop(0, NC, step, 0)

    for phase in range(4):
        settle(phase)
    for slot in range(2):
        i = mine + 32 * slot

        @pl.when(i < 4 * CH)
        def _():
            landed(gout.at[slot, pl.ds(0, 31)], bs.at[slot])

    two = mine + 32 < 4 * CH

    @pl.when(two)
    def _():
        landed(hid.at[pl.ds(0, 4 * CH - 2)], as_.at[0])

    @pl.when(jnp.logical_not(two))
    def _():
        landed(hid.at[pl.ds(0, 4 * CH - 1)], as_.at[0])


def per_device(
    tokens, gate_codes, gate_scales, up_codes, up_scales, down_codes, down_scales, flip_signs
):
    vm = pl.BlockSpec(memory_space=pltpu.VMEM)
    hbm = pl.BlockSpec(memory_space=pl.ANY)
    dma = pltpu.SemaphoreType.DMA
    ng = len(GROUPS)
    return pl.pallas_call(
        kernel,
        out_shape=jax.ShapeDtypeStruct((16, 2048), BF16),
        in_specs=[vm, hbm, hbm, hbm, vm, vm, vm, vm, hbm],
        out_specs=vm,
        scratch_shapes=[
            pltpu.VMEM((512, 2048), jnp.int32),
            pltpu.VMEM((512, 1664), jnp.int32),
            pltpu.VMEM((CH, 2048, 256), BF16),
            pltpu.VMEM((2, 8, 2, 16, 2048), BF16),
            pltpu.VMEM((CH, 4, 2, 64, 256), BF16),
            pltpu.VMEM((CH, 2, 64, 256), BF16),
            pltpu.VMEM((CH, 2, 2, 64, 256), BF16),
            pltpu.VMEM((CH, 4, 64, 256), BF16),
            pltpu.VMEM((CH, 64, 256), BF16),
            pltpu.VMEM((CH, 64, 256), BF16),
            pltpu.VMEM((CH, 64, 256), F32),
            pltpu.VMEM((1664, 1664), BF16),
            pltpu.VMEM((4 * CH, 16, 128), BF16),
            pltpu.VMEM((2, 32, 16, 128), BF16),
            pltpu.VMEM((2, 32, 16, 128), BF16),
            pltpu.VMEM((8, 64, 1664), BF16),
            pltpu.VMEM((512, 2048), F32),
            pltpu.VMEM((1664, 2048), BF16),
            pltpu.VMEM((NC, 2, 2, 8, 16, WC), BF16),
            pltpu.VMEM((NC, 2, 8, 16, WC), BF16),
            pltpu.VMEM((NC, 2, 16, WC), BF16),
            pltpu.VMEM((3, NC, 2, 2, 16, WC), BF16),
            pltpu.VMEM((NC, 16, WC), BF16),
            dma((4,)), dma((4,)), dma((1,)), dma((2,)), dma((2,)), dma((ng,)), dma((1,)),
            dma((8, 2)), dma((4, 2, 2)), dma((3, 2, 2)), dma((CH,)), dma((CH,)), dma((CH,)), dma((ng, 4)),
            dma((NC,)), dma((4, NC)), dma((NC,)),
        ],
        compiler_params=pltpu.CompilerParams(
            collective_id=0, has_side_effects=True, vmem_limit_bytes=VMEM_LIMIT
        ),
        cost_estimate=pl.CostEstimate(flops=14 * 10**9, bytes_accessed=2 * 10**7, transcendentals=10**5),
    )(
        tokens, gate_codes, up_codes, down_codes, gate_scales, up_scales, down_scales,
        flip_signs, jnp.asarray(inner_table(), dtype=BF16),
    )


def solution(mesh):
    return jax.shard_map(
        per_device,
        mesh=mesh,
        in_specs=(
            P("tensor", "dp"),
            P("dp", "tensor"),
            P("dp", "tensor"),
            P("dp", "tensor"),
            P("dp", "tensor"),
            P("tensor", "dp"),
            P("tensor", "dp"),
            P("tensor"),
        ),
        out_specs=P("tensor", "dp"),
        check_vma=False,
    )
```

time: 124 us -> 106 us (0.85)
  Pallas kernels: 121 us -> 103 us
    pallas_call x1, Pallas kernels: 121 us -> 103 us  [per_device(): pl.pallas_call(kernel, out_shape=jax.ShapeDtypeStruct((16, 2048), BF16),...]
where the time goes in v3:
time: 106 us; the launch traced here: 105 us
  Pallas kernels  103 us (97%)
  local copies, waits for them, and re-layouts  1.47 us (1%)
    pallas_call x1, Pallas kernels, per_device(): pl.pallas_call(kernel, out_shape=jax.ShapeDtypeStruct((16, 2048), BF16),...  103 us

profile of v3, /device:TPU:2, one launch (start us, length us, event | category | flops | bytes accessed | tf_op | source)
XLA Modules:
  0.0 104.8 jit_solution(11055109587296332796)
XLA Ops:
  0.0 103.3 %shard_map.91 = bf16[16,2048]{1,0:T(8,128)(2,1)} custom-call(bf16[16,2048]{1,0:T(8,128)(2,1)} %tok.1, s32[512,1664]{1,0:T(8,128)} %gcodes.1, s32[512,1664]{1,0:T(8,128)} %ucodes.1, s32[416,2048]{1,0:T(8,128)} %dcodes.1, bf16[16,1664]{1,0:T(8,128)(2,1)} %gs.1, bf16[16,1664]{1,0:T(8,128)(2,1)} %us.1, bf16[13,2048]{1,0:T(8,128)(2,1)} %ds_.1, s32[1664]{0:T(1024)} %flip.1, ...), custom_call_target="tpu_custom_call" | custom-call | flops 14000000000 | bytes 20000000 | tf_op jit(solution)/shard_map/pallas_call | solution.py:608
  103.3 1.5 %copy.11 = bf16[16,2048]{1,0:T(8,128)(2,1)} copy(bf16[16,2048]{1,0:T(8,128)(2,1)} %shard_map.91) | data formatting | bytes 131072

commit v4 on v3

--- a/solution.py
+++ b/solution.py
@@ -77,8 +77,8 @@
 
 
 CH = 13
-GROUPS = ((0, 3, False, "2"), (3, 3, True, "y"), (6, 3, False, "y"), (9, 4, True, "x"))
-ORDER = (1, 0, 2, 3)
+GROUPS = ((0, 2, True, "y"), (2, 3, True, "2"), (5, 4, False, "y"), (9, 4, True, "y"))
+EARLY = 2
 NC = 4
 WC = 512
 
@@ -119,12 +119,12 @@
     load_g.start()
     load_u.start()
 
-    rows_i = lax.broadcasted_iota(jnp.int32, (512, 512), 0)
-    cols_i = lax.broadcasted_iota(jnp.int32, (512, 512), 1)
-    pick = jnp.where(rows_i == 4 * (cols_i % 128) + cols_i // 128, 1.0, 0.0).astype(BF16)
+    apart = lax.broadcasted_iota(jnp.int32, (512, 128), 0) - 4 * lax.broadcasted_iota(jnp.int32, (512, 128), 1)
+    pick = jnp.concatenate([jnp.where(apart == j, 1.0, 0.0).astype(BF16) for j in range(4)], axis=1)
+    stacked = jnp.concatenate([tok[:, 512 * q : 512 * q + 512] for q in range(4)], axis=0)
+    placed = jnp.dot(stacked, pick, preferred_element_type=F32).astype(BF16)
     for q in range(4):
-        cols = slice(512 * q, 512 * q + 512)
-        xg[yl, z, core, :, cols] = jnp.dot(tok[:, cols], pick, preferred_element_type=F32).astype(BF16)
+        xg[yl, z, core, :, 512 * q : 512 * q + 512] = placed[16 * q : 16 * q + 16]
 
     pl.semaphore_wait(barrier, 34)
 
@@ -460,19 +460,18 @@
             product = jnp.dot(table[rows, :], wd[:, cols], preferred_element_type=F32)
             w[n, rows] = (product * FF**-0.5).astype(BF16)
 
-    def terms_of(g, n):
-        first, count = GROUPS[g][:2]
-        rows = pl.ds(128 * first, 128 * count)
-        units = rg[:, :, 128 * first : 128 * (first + count)].reshape(512, 128 * count)
-        return jnp.dot(units, w[n, rows], preferred_element_type=F32)
-
-    def accumulate(g):
-        gather_wait(g)
+    def terms_of(first, stop, n):
+        units = rg[:, :, 128 * first : 128 * stop].reshape(512, 128 * (stop - first))
+        return jnp.dot(units, w[n, pl.ds(128 * first, 128 * (stop - first))], preferred_element_type=F32)
+
+    split = GROUPS[EARLY][0]
+
+    def accumulate():
+        for g in range(EARLY):
+            gather_wait(g)
 
         def step(n, carry):
-            cols = pl.ds(pl.multiple_of(256 * n, 256), 256)
-            terms = terms_of(g, n)
-            acc[:, cols] = terms if g == ORDER[0] else acc[:, cols] + terms
+            acc[:, pl.ds(pl.multiple_of(256 * n, 256), 256)] = terms_of(0, split, n)
             return carry
 
         lax.fori_loop(0, 8, step, 0)
@@ -502,10 +501,11 @@
         load_d.wait()
         lax.fori_loop(0, 16, dequant_down, 0)
 
-    M(0), M(1), M(3), S2(1), M(2), S2(0), S2(3)
+    M(0), M(3), S2(0), M(2), M(1), S2(3), S3(0)
     unpack_down()
-    W(0), S3(1), S3(0), W(1), W(2), S2(2), S3(3), W(3), S4(1), S4(0), S3(2), S4(3), S4(2), H(1), H(0), H(3), H(2)
-    T1(1), T1(0), W(4), T2(1), T1(2), T1(3), W(5), T2(0), W(6), T3(1), T2(2), W(7), T2(3), A(1), T3(2), T3(3), A(0), A(2)
+    W(0), W(1), S2(1), W(2), S3(3), S4(0), S2(2), S3(1), S4(3), S3(2), W(3), S4(1), H(0), S4(2), H(3), H(1)
+    T1(0), W(4), H(2), T1(3), T2(0), T1(1), T1(2), T2(3), W(5), T3(0), T2(1), W(6), T2(2), T3(3), W(7), T3(2)
+    A()
 
     def pair(c):
         push(3, qb.at[c, co], rc.at[c], ccr.at[c], dev_c, NC).start()
@@ -516,10 +516,10 @@
         push(3, qb.at[c, core, yo, z], rl.at[c], yyr.at[c], dev_y, times).start()
 
     def down(c):
-        for part in range(2):
-            n = 2 * c + part
+        for part in range(WC // 256):
+            n = WC // 256 * c + part
             cols = pl.ds(pl.multiple_of(256 * n, 256), 256)
-            terms = (acc[:, cols] + terms_of(ORDER[-1], n)).astype(BF16)
+            terms = (acc[:, cols] + terms_of(split, CH, n)).astype(BF16)
             for cc in range(2):
                 for yy in range(2):
                     for zz in range(8):
@@ -562,7 +562,8 @@
         out[:, cols] = total.astype(BF16)
         return carry
 
-    gather_wait(ORDER[-1])
+    for g in range(EARLY, len(GROUPS)):
+        gather_wait(g)
 
     def start(c, carry):
         down(c)

time: 106 us -> 104 us (0.981)
  Pallas kernels: 103 us -> 101 us
    pallas_call x1, Pallas kernels: 103 us -> 101 us  [per_device(): pl.pallas_call(kernel, out_shape=jax.ShapeDtypeStruct((16, 2048), BF16),...]
where the time goes in v4:
time: 104 us; the launch traced here: 103 us
  Pallas kernels  101 us (97%)
  local copies, waits for them, and re-layouts  1.47 us (1%)
    pallas_call x1, Pallas kernels, per_device(): pl.pallas_call(kernel, out_shape=jax.ShapeDtypeStruct((16, 2048), BF16),...  101 us

profile of v4, /device:TPU:2, one launch (start us, length us, event | category | flops | bytes accessed | tf_op | source)
XLA Modules:
  0.0 102.9 jit_solution(15334638130718300775)
XLA Ops:
  0.0 101.4 %shard_map.91 = bf16[16,2048]{1,0:T(8,128)(2,1)} custom-call(bf16[16,2048]{1,0:T(8,128)(2,1)} %tok.1, s32[512,1664]{1,0:T(8,128)} %gcodes.1, s32[512,1664]{1,0:T(8,128)} %ucodes.1, s32[416,2048]{1,0:T(8,128)} %dcodes.1, bf16[16,1664]{1,0:T(8,128)(2,1)} %gs.1, bf16[16,1664]{1,0:T(8,128)(2,1)} %us.1, bf16[13,2048]{1,0:T(8,128)(2,1)} %ds_.1, s32[1664]{0:T(1024)} %flip.1, ...), custom_call_target="tpu_custom_call" | custom-call | flops 14000000000 | bytes 20000000 | tf_op jit(solution)/shard_map/pallas_call | solution.py:609
  101.4 1.5 %copy.11 = bf16[16,2048]{1,0:T(8,128)(2,1)} copy(bf16[16,2048]{1,0:T(8,128)(2,1)} %shard_map.91) | data formatting | bytes 131072

commit v5 on v4

--- a/solution.py
+++ b/solution.py
@@ -103,14 +103,8 @@
     dev_r, dev_l, dev_h = (xr * 2 + yh, t), (xl * 2 + yh, t), (x * 2 + ho, t)
 
     barrier = pltpu.get_barrier_semaphore()
-    for device in (dev_r, dev_l, dev_h):
+    for device in (dev_r, dev_l, dev_h, dev_y, dev_c, dev_p, dev_s):
         pl.semaphore_signal(barrier, inc=1, device_id=device, device_id_type=MESH)
-
-    def greet(k, carry):
-        pl.semaphore_signal(barrier, inc=1, device_id=(dp, lax.rem(t + k, 32)), device_id_type=MESH)
-        return carry
-
-    lax.fori_loop(1, 32, greet, 0)
     gbuf, dbuf = cbuf.at[:, pl.ds(0, 1664)], cbuf.at[pl.ds(0, 416)]
     load_g = pltpu.make_async_copy(gcodes, gbuf, ld.at[0])
     load_u = pltpu.make_async_copy(ucodes, ubuf, ld.at[1])
@@ -126,7 +120,7 @@
     for q in range(4):
         xg[yl, z, core, :, 512 * q : 512 * q + 512] = placed[16 * q : 16 * q + 16]
 
-    pl.semaphore_wait(barrier, 34)
+    pl.semaphore_wait(barrier, 7)
 
     sent = [0, 0, 0, 0]
 

time: 104 us -> 102 us (0.981)
    pallas_call x1, Pallas kernels: 101 us -> 100 us  [per_device(): pl.pallas_call(kernel, out_shape=jax.ShapeDtypeStruct((16, 2048), BF16),...]
where the time goes in v5:
time: 102 us
  Pallas kernels  100 us (98%)
  local copies, waits for them, and re-layouts  1.47 us (1%)
    pallas_call x1, Pallas kernels, per_device(): pl.pallas_call(kernel, out_shape=jax.ShapeDtypeStruct((16, 2048), BF16),...  100 us

profile of v5, /device:TPU:2, one launch (start us, length us, event | category | flops | bytes accessed | tf_op | source)
XLA Modules:
  0.0 101.8 jit_solution(11915875190488459650)
XLA Ops:
  0.0 100.3 %shard_map.91 = bf16[16,2048]{1,0:T(8,128)(2,1)} custom-call(bf16[16,2048]{1,0:T(8,128)(2,1)} %tok.1, s32[512,1664]{1,0:T(8,128)} %gcodes.1, s32[512,1664]{1,0:T(8,128)} %ucodes.1, s32[416,2048]{1,0:T(8,128)} %dcodes.1, bf16[16,1664]{1,0:T(8,128)(2,1)} %gs.1, bf16[16,1664]{1,0:T(8,128)(2,1)} %us.1, bf16[13,2048]{1,0:T(8,128)(2,1)} %ds_.1, s32[1664]{0:T(1024)} %flip.1, ...), custom_call_target="tpu_custom_call" | custom-call | flops 14000000000 | bytes 20000000 | tf_op jit(solution)/shard_map/pallas_call | solution.py:603
  100.3 1.5 %copy.11 = bf16[16,2048]{1,0:T(8,128)(2,1)} copy(bf16[16,2048]{1,0:T(8,128)(2,1)} %shard_map.91) | data formatting | bytes 131072
